TPU v7x, 32 devices: a whole 2x2x4 slice. The times are simulated.
32 devices in a mesh: dp: 4 (over z), pipe: 2 (over core), space: 4 (over y, x).
Axes of the slice: x: 2, y: 2, z: 4, core: 2. Of those that a mesh axis runs over, the one named last changes fastest.
Arguments:
- edges: bfloat16 [2, 8, 192, 384, 256], P('pipe', 'dp', 'space'), may hold values from -6 to 6
- mask_levels: int32 [192, 384, 256], P('space'), may hold values from 0 to 1, as said below
- norm_gains: float32 [2, 2, 256], P('pipe'), may hold values from 0.5 to 1.5
- norm_biases: float32 [2, 2, 256], P('pipe'), may hold values from -1.5 to 1.5
- filters: float32 [2, 2, 192, 256], P('pipe'), may hold values from -4 to 4
- w_in: bfloat16 [2, 256, 512], P('pipe'), may hold values from -0.375 to 0.375
- bias_in: float32 [2, 512], P('pipe'), may hold values from -1.5 to 1.5
- w_out: bfloat16 [2, 512, 256], P('pipe'), may hold values from -0.375 to 0.375
- bias_out: float32 [2, 256], P('pipe'), may hold values from -1.5 to 1.5
Outputs:
- ends: float32 [2, 8, 192, 384, 256], P('pipe', 'dp', 'space')
- grad_gains: float32 [2, 2, 256], P('pipe', None, 'space')
- grad_biases: float32 [2, 2, 256], P('pipe', None, 'space')
- grad_filters: float32 [2, 2, 192, 256], P('pipe', None, None, 'space')
- grad_w_in: float32 [2, 256, 512], P('pipe', 'space')
- grad_bias_in: float32 [2, 512], P('pipe', 'space')
- grad_w_out: float32 [2, 512, 256], P('pipe', 'space')
- grad_bias_out: float32 [2, 256], P('pipe', 'space')
Inputs may be any that keep to these rules, and one draw needn't show every extreme that they name: `mask_levels`: each point has a ground level of 0 to 6, or 8; channel c of the point is live (1) exactly where c mod 8 is at least that level, so a point with level 8 has no live channel.
All inputs are finite; a program needn't handle non-finite values.
Results may differ from a plain program's by a relative error of at most 0.025.
Values may be sent and summed in bfloat16 or wider, within the bound.
A program may use at most 896 MiB of HBM per device.

v0:
```python
from functools import partial
import math

import jax
import jax.numpy as jnp
from jax import lax
from jax.sharding import PartitionSpec as P

NORM_EPS = 1e-05


def swapped(value, axis, bit):
    mask = 2**bit
    pairs = [(source, source ^ mask) for source in range(lax.axis_size(axis))]
    return lax.ppermute(value, axis, pairs)


def for_sending(shard):
    return jax.tree.map(lambda a: a.astype(jnp.bfloat16) if a.dtype == jnp.float32 else a, shard)


def legendre_table(orders, degree_count, colat_count):
    colatitude = (jnp.arange(colat_count, dtype=jnp.float32) + 0.5) * (math.pi / colat_count)
    cosine = jnp.cos(colatitude)
    sine_col = jnp.sin(colatitude)
    order_value = orders.astype(jnp.float32)[:, None]
    log_start = (
        0.5
        * (
            jnp.log((2.0 * order_value + 1.0) / (4.0 * math.pi))
            + lax.lgamma(order_value + 0.5)
            - lax.lgamma(order_value + 1.0)
            - 0.5 * math.log(math.pi)
        )
        + order_value * jnp.log(sine_col)[None, :]
    )
    start_row = jnp.exp(log_start)

    def recurrence(pair_carry, degree):
        older_row, newer_row = pair_carry
        degree_value = degree.astype(jnp.float32)
        ahead_coef = jnp.sqrt(
            jnp.maximum(4.0 * degree_value * degree_value - 1.0, 0.0)
            / jnp.maximum(degree_value * degree_value - order_value * order_value, 1.0)
        )
        degree_below = degree_value - 1.0
        behind = jnp.sqrt(
            jnp.maximum(degree_below * degree_below - order_value * order_value, 0.0)
            / jnp.maximum(4.0 * degree_below * degree_below - 1.0, 1.0)
        )
        general = ahead_coef * (cosine * newer_row - behind * older_row)
        table_value = jnp.where(
            degree_value < order_value,
            0.0,
            jnp.where(degree_value == order_value, start_row, general),
        )
        return ((newer_row, table_value), table_value)

    zero_rows = jnp.zeros((orders.shape[0], colat_count), jnp.float32)
    last_pair, table_rows = lax.scan(
        recurrence, (zero_rows, zero_rows), jnp.arange(degree_count, dtype=jnp.int32)
    )
    return (jnp.transpose(table_rows, (1, 0, 2)), sine_col)


def fourier_tables(order_count, lon_count):
    orders = jnp.arange(order_count, dtype=jnp.int32)
    points = jnp.arange(lon_count, dtype=jnp.int32)
    phase_index = orders[:, None] * points[None, :] % lon_count
    angle_value = phase_index.astype(jnp.float32) * (2.0 * math.pi / lon_count)
    dft_scale = 2.0 * math.pi / lon_count
    forward = jnp.stack(
        [jnp.cos(angle_value) * dft_scale, -jnp.sin(angle_value) * dft_scale], axis=1
    ).reshape(2 * order_count, lon_count)
    double = jnp.where(orders == 0, 1.0, 2.0).astype(jnp.float32)[:, None]
    inverse = jnp.stack(
        [jnp.cos(angle_value) * double, -jnp.sin(angle_value) * double], axis=1
    ).reshape(2 * order_count, lon_count)
    return (forward, jnp.transpose(inverse))


def norm_masked(values, live_mask, norm_gain, norm_bias):
    live_count = jnp.maximum(jnp.sum(live_mask, axis=-1, keepdims=True), 1.0)
    average = jnp.sum(live_mask * values, axis=-1, keepdims=True) / live_count
    centered = live_mask * (values - average)
    spread = jnp.sum(centered * centered, axis=-1, keepdims=True) / live_count
    return centered * lax.rsqrt(spread + NORM_EPS) * norm_gain + live_mask * norm_bias


def norm_plain(values, norm_gain, norm_bias):
    average = jnp.mean(values, axis=-1, keepdims=True)
    centered = values - average
    spread = jnp.mean(centered * centered, axis=-1, keepdims=True)
    return centered * lax.rsqrt(spread + NORM_EPS) * norm_gain + norm_bias


def filter_modes(coefficients, filter_real, filter_imag):
    real_part = coefficients[:, :, 0]
    imag_part = coefficients[:, :, 1]
    return jnp.stack(
        [
            real_part * filter_real - imag_part * filter_imag,
            real_part * filter_imag + imag_part * filter_real,
        ],
        axis=2,
    )


def split_pairs(moved_data):
    return moved_data.reshape(moved_data.shape[0], moved_data.shape[1] // 2, 2, moved_data.shape[2])


def join_pairs(modal_data):
    return modal_data.reshape(modal_data.shape[0], modal_data.shape[1] * 2, modal_data.shape[3])


def to_modes(spectrum):
    moved_data = lax.all_to_all(spectrum, "space", split_axis=1, concat_axis=0, tiled=True)
    return split_pairs(moved_data)


def to_bands(modal_data):
    joined = join_pairs(modal_data)
    return lax.all_to_all(joined, "space", split_axis=0, concat_axis=1, tiled=True)


def grad_to_modes(spectrum):
    moved_data = lax.all_to_all(spectrum, "space", split_axis=1, concat_axis=0, tiled=True)
    return split_pairs(moved_data)


def grad_to_bands(modal_data):
    joined = join_pairs(modal_data)
    return lax.all_to_all(joined, "space", split_axis=0, concat_axis=1, tiled=True)


def local(edges, mask_levels, norm_gains, norm_biases, filters, w_in, bias_in, w_out, bias_out):
    section_index = lax.axis_index("pipe")
    band_count = lax.axis_size("space")
    micro_count = edges.shape[1]
    lon_count = edges.shape[3]
    channel_count = edges.shape[4]
    lat_count = edges.shape[2] * band_count
    order_count = lon_count // 2
    live_mask = mask_levels.astype(jnp.float32)
    forward_table, inverse_table = fourier_tables(order_count, lon_count)
    forward_dft = forward_table.astype(jnp.bfloat16)
    inverse_dft = inverse_table.astype(jnp.bfloat16)
    order_dev = order_count // band_count
    orders = lax.axis_index("space") * order_dev + jnp.arange(order_dev, dtype=jnp.int32)
    legendre, sine_col = legendre_table(orders, lat_count, lat_count)
    analysis = (legendre * (sine_col * (math.pi / lat_count))[None, None, :]).astype(jnp.bfloat16)
    synthesis = legendre.astype(jnp.bfloat16)
    gelu_tanh = partial(jax.nn.gelu, approximate=True)

    def filter_parts(filter_pair):
        return (filter_pair[0], filter_pair[1])

    def first_norm(values, norm_gain, norm_bias):
        return norm_masked(values, live_mask, norm_gain, norm_bias)

    def forward_layer(values, params):
        gain_pair, bias_pair, filter_pair, weight_in, shift_in, weight_out, shift_out = params
        filter_real, filter_imag = filter_parts(filter_pair)
        normed = first_norm(values, gain_pair[0], bias_pair[0]).astype(jnp.bfloat16)
        spectrum = jnp.einsum(
            "kw,hwc->hkc", forward_dft, normed, preferred_element_type=jnp.float32
        ).astype(jnp.bfloat16)
        modal_data = to_modes(spectrum)
        coefficients = jnp.einsum(
            "mlh,hmrc->mlrc", analysis, modal_data, preferred_element_type=jnp.float32
        )
        filtered = filter_modes(coefficients, filter_real, filter_imag).astype(jnp.bfloat16)
        synthesized = jnp.einsum(
            "mlh,mlrc->hmrc", synthesis, filtered, preferred_element_type=jnp.float32
        ).astype(jnp.bfloat16)
        banded = to_bands(synthesized)
        mixed_grid = jnp.einsum(
            "wk,hkc->hwc", inverse_dft, banded, preferred_element_type=jnp.float32
        )
        residual = values + mixed_grid
        normed_two = (
            norm_plain(residual, gain_pair[1], bias_pair[1])
            .astype(jnp.bfloat16)
            .reshape(-1, channel_count)
        )
        hidden = jnp.dot(normed_two, weight_in, preferred_element_type=jnp.float32) + shift_in
        active = gelu_tanh(hidden).astype(jnp.bfloat16)
        output = jnp.dot(active, weight_out, preferred_element_type=jnp.float32) + shift_out
        saved_state = (values, coefficients, residual, hidden)
        return (residual + output.reshape(values.shape), saved_state)

    def backward_layer(grad_out, saved_state, params):
        gain_pair, bias_pair, filter_pair, weight_in, shift_in, weight_out, shift_out = params
        filter_real, filter_imag = filter_parts(filter_pair)
        values, coefficients, residual, hidden = saved_state
        normed_two_full, norm_two_pull = jax.vjp(norm_plain, residual, gain_pair[1], bias_pair[1])
        normed_two = normed_two_full.astype(jnp.bfloat16).reshape(-1, channel_count)
        active_full, gelu_pull = jax.vjp(gelu_tanh, hidden)
        active = active_full.astype(jnp.bfloat16)
        flat_grad = grad_out.reshape(-1, channel_count)
        grad_shift_out = jnp.sum(flat_grad, axis=0)
        grad_low = flat_grad.astype(jnp.bfloat16)
        grad_weight_out = jnp.einsum(
            "pf,pc->fc", active, grad_low, preferred_element_type=jnp.float32
        )
        grad_active = jnp.einsum(
            "pc,fc->pf", grad_low, weight_out, preferred_element_type=jnp.float32
        )
        grad_hidden = gelu_pull(grad_active)[0]
        grad_shift_in = jnp.sum(grad_hidden, axis=0)
        hidden_low = grad_hidden.astype(jnp.bfloat16)
        grad_weight_in = jnp.einsum(
            "pc,pf->cf", normed_two, hidden_low, preferred_element_type=jnp.float32
        )
        grad_normed_two = jnp.einsum(
            "pf,cf->pc", hidden_low, weight_in, preferred_element_type=jnp.float32
        )
        grad_norm_res, grad_gain_two, grad_bias_two = norm_two_pull(
            grad_normed_two.reshape(residual.shape)
        )
        grad_residual = grad_out + grad_norm_res
        mixed_low = grad_residual.astype(jnp.bfloat16)
        grad_banded = jnp.einsum(
            "wk,hwc->hkc", inverse_dft, mixed_low, preferred_element_type=jnp.float32
        ).astype(jnp.bfloat16)
        grad_modal = grad_to_modes(grad_banded)
        grad_filtered = jnp.einsum(
            "mlh,hmrc->mlrc", synthesis, grad_modal, preferred_element_type=jnp.float32
        )
        filtered_full, filter_pull = jax.vjp(filter_modes, coefficients, filter_real, filter_imag)
        grad_coefficients, grad_filter_real, grad_filter_imag = filter_pull(grad_filtered)
        grad_spectrum = jnp.einsum(
            "mlh,mlrc->hmrc",
            analysis,
            grad_coefficients.astype(jnp.bfloat16),
            preferred_element_type=jnp.float32,
        ).astype(jnp.bfloat16)
        grad_lat = grad_to_bands(grad_spectrum)
        grad_normed = jnp.einsum(
            "kw,hkc->hwc", forward_dft, grad_lat, preferred_element_type=jnp.float32
        )
        normed_full, norm_one_pull = jax.vjp(first_norm, values, gain_pair[0], bias_pair[0])
        grad_norm_in, grad_gain_one, grad_bias_one = norm_one_pull(grad_normed)
        grad_values = grad_residual + grad_norm_in
        layer_grads = (
            jnp.stack([grad_gain_one, grad_gain_two]),
            jnp.stack([grad_bias_one, grad_bias_two]),
            jnp.stack([grad_filter_real, grad_filter_imag]),
            grad_weight_in,
            grad_shift_in,
            grad_weight_out,
            grad_shift_out,
        )
        return (grad_values, layer_grads)

    gathered = (
        lax.all_gather(norm_gains.astype(jnp.bfloat16), "pipe", axis=0, tiled=True).astype(
            norm_gains.dtype
        ),
        lax.all_gather(norm_biases.astype(jnp.bfloat16), "pipe", axis=0, tiled=True).astype(
            norm_biases.dtype
        ),
        lax.all_gather(filters.astype(jnp.bfloat16), "pipe", axis=0, tiled=True).astype(
            filters.dtype
        ),
        lax.all_gather(
            w_in.astype(jnp.float32).astype(jnp.bfloat16), "pipe", axis=0, tiled=True
        ).astype(jnp.float32),
        lax.all_gather(bias_in.astype(jnp.bfloat16), "pipe", axis=0, tiled=True).astype(
            bias_in.dtype
        ),
        lax.all_gather(
            w_out.astype(jnp.float32).astype(jnp.bfloat16), "pipe", axis=0, tiled=True
        ).astype(jnp.float32),
        lax.all_gather(bias_out.astype(jnp.bfloat16), "pipe", axis=0, tiled=True).astype(
            bias_out.dtype
        ),
    )
    all_gains, all_biases, all_filters, all_win, all_bin, all_wout, all_bout = gathered
    layer_params = [
        (
            all_gains[layer_number],
            all_biases[layer_number],
            all_filters[layer_number],
            all_win[layer_number].astype(jnp.bfloat16),
            all_bin[layer_number],
            all_wout[layer_number].astype(jnp.bfloat16),
            all_bout[layer_number],
        )
        for layer_number in range(2)
    ]
    half_count = micro_count // 2
    sending = jnp.where(section_index == 0, edges[0, half_count:], edges[0, :half_count])
    arrived = swapped(sending, "pipe", 0)
    my_inputs = jnp.where(section_index == 0, edges[0, :half_count], arrived)
    my_cotangents = jnp.where(section_index == 0, arrived, edges[0, half_count:])
    first_out, first_state = forward_layer(my_inputs[0].astype(jnp.float32), layer_params[0])
    second_out, second_state = forward_layer(first_out, layer_params[1])
    output_list = [second_out]
    grad_middle, grads_second = backward_layer(
        my_cotangents[0].astype(jnp.float32), second_state, layer_params[1]
    )
    grad_start, grads_first = backward_layer(grad_middle, first_state, layer_params[0])
    grad_list = [grad_start]
    stacked = tuple(
        (
            jnp.stack([first_entry, second_entry])
            for first_entry, second_entry in zip(grads_first, grads_second)
        )
    )
    mine = (
        lax.psum_scatter(
            stacked[0].astype(jnp.bfloat16), "pipe", scatter_dimension=0, tiled=True
        ).astype(jnp.float32),
        lax.psum_scatter(
            stacked[1].astype(jnp.bfloat16), "pipe", scatter_dimension=0, tiled=True
        ).astype(jnp.float32),
        lax.psum_scatter(
            stacked[2].astype(jnp.bfloat16), "pipe", scatter_dimension=0, tiled=True
        ).astype(jnp.float32),
        lax.psum_scatter(
            stacked[3].astype(jnp.bfloat16), "pipe", scatter_dimension=0, tiled=True
        ).astype(jnp.float32),
        lax.psum_scatter(
            stacked[4].astype(jnp.bfloat16), "pipe", scatter_dimension=0, tiled=True
        ).astype(jnp.float32),
        lax.psum_scatter(
            stacked[5].astype(jnp.bfloat16), "pipe", scatter_dimension=0, tiled=True
        ).astype(jnp.float32),
        lax.psum_scatter(
            stacked[6].astype(jnp.bfloat16), "pipe", scatter_dimension=0, tiled=True
        ).astype(jnp.float32),
    )
    totals = tuple((entry[0] for entry in mine))
    output_half = jnp.stack(output_list)
    grad_half = jnp.stack(grad_list)
    reply = jnp.where(section_index == 0, output_half, grad_half)
    returned = swapped(for_sending(reply), "pipe", 0).astype(reply.dtype)
    ends = jnp.where(
        section_index == 0,
        jnp.concatenate([grad_half, returned], axis=0),
        jnp.concatenate([returned, output_half], axis=0),
    )[None]
    gain_grads, bias_grads, filter_grads, win_grads, bin_grads, wout_grads, bout_grads = totals
    gain_part, bias_part, filter_part, win_part, bin_part, wout_part, bout_part = (
        lax.psum_scatter(
            gain_grads.astype(jnp.bfloat16), "space", scatter_dimension=1, tiled=True
        ).astype(jnp.float32),
        lax.psum_scatter(
            bias_grads.astype(jnp.bfloat16), "space", scatter_dimension=1, tiled=True
        ).astype(jnp.float32),
        lax.psum_scatter(
            filter_grads.astype(jnp.bfloat16), "space", scatter_dimension=2, tiled=True
        ).astype(jnp.float32),
        lax.psum_scatter(
            win_grads.astype(jnp.bfloat16), "space", scatter_dimension=0, tiled=True
        ).astype(jnp.float32),
        lax.psum_scatter(
            bin_grads.astype(jnp.bfloat16), "space", scatter_dimension=0, tiled=True
        ).astype(jnp.float32),
        lax.psum_scatter(
            wout_grads.astype(jnp.bfloat16), "space", scatter_dimension=0, tiled=True
        ).astype(jnp.float32),
        lax.psum_scatter(
            bout_grads.astype(jnp.bfloat16), "space", scatter_dimension=0, tiled=True
        ).astype(jnp.float32),
    )
    summed = (
        lax.psum(gain_part.astype(jnp.bfloat16), "dp").astype(jnp.float32),
        lax.psum(bias_part.astype(jnp.bfloat16), "dp").astype(jnp.float32),
        lax.psum(filter_part.astype(jnp.bfloat16), "dp").astype(jnp.float32),
        lax.psum(win_part.astype(jnp.bfloat16), "dp").astype(jnp.float32),
        lax.psum(bin_part.astype(jnp.bfloat16), "dp").astype(jnp.float32),
        lax.psum(wout_part.astype(jnp.bfloat16), "dp").astype(jnp.float32),
        lax.psum(bout_part.astype(jnp.bfloat16), "dp").astype(jnp.float32),
    )
    return (ends,) + tuple((entry[None] for entry in summed))


def solution(mesh):
    return jax.shard_map(
        local,
        mesh=mesh,
        in_specs=(
            P("pipe", "dp", "space", None, None),
            P("space", None, None),
            P("pipe", None, None),
            P("pipe", None, None),
            P("pipe", None, None, None),
            P("pipe", None, None),
            P("pipe", None),
            P("pipe", None, None),
            P("pipe", None),
        ),
        out_specs=(
            P("pipe", "dp", "space", None, None),
            P("pipe", None, "space"),
            P("pipe", None, "space"),
            P("pipe", None, None, "space"),
            P("pipe", "space", None),
            P("pipe", "space"),
            P("pipe", "space", None),
            P("pipe", "space"),
        ),
        check_vma=False,
    )
```

profile of v0, /device:TPU:0, one launch (start us, length us, event | category | flops | bytes accessed | tf_op | source)
XLA Modules:
  0.0 2713.2 jit_solution(15256802936412774838)
XLA Ops:
  7.2 14.3 fusion.156
  34.1 12.7 copy.443
  60.3 18.8 copy.347
  84.0 14.2 convert_reduce_fusion
  102.9 14.7 convert_bitcast_fusion.3
  117.6 13.0 copy.349
  136.3 397.2 %while.20 = (s32[]{:T(128)}, f32[48,192]{1,0:T(8,128)S(1)}, f32[48,192]{1,0:T(8,128)S(1)}, f32[192,48,192]{2,1,0:T(8,128)}, s32[192]{0:T(256)S(1)}, /*index=5*/s...) while((s32[]{:T(128)}, f32[48,192]{1,0:T(8,128)S(1)}, ...), condition=%wide.region_1.2_spmd.clone.clone.clone, body=%wide.region_0.1_spmd.clone.clone.clone.sunk | while | flops 83967 | bytes 200599 | solution.py:60
  538.2 12.7 convert_bitcast_fusion.5
  575.5 14.2 fusion.165
  605.5 12.7 copy.358
  635.0 94.5 %all-to-all-done.1 = bf16[192,96,256]{2,1,0:T(8,128)(2,1)} async-done(((bf16[192,96,256]{2,1,0:T(8,128)(2,1)}), bf16[192,96,256]{2,1,0:T(8,128)(2,1)}, u32[]{:S(2)}, u32[]{:S(2)}) %all-to-all-start.1) | async-done | bytes 9437216 | tf_op jit(solution)/shard_map/all_to_all | solution.py:124
  738.2 14.1 fusion.161
  785.4 25.5 multiply_convert_fusion.1
  810.9 12.9 convolution_add_fusion.1
  823.8 18.7 copy.363
  842.5 18.3 multiply_reduce_fusion.8
  860.8 21.1 multiply_reduce_fusion.7
  882.5 18.8 convert_bitcast_fusion.2
  901.4 13.2 copy.364
  914.6 112.6 %all_to_all.132 = bf16[48,384,256]{2,0,1:T(8,128)(2,1)} all-to-all(bf16[48,384,256]{2,0,1:T(8,128)(2,1)} %copy.364), channel_id=1, replica_groups=mesh['dp'=4,'pipe'=2,'space'=4] {'space'}, dimensions={1} | all-to-all | bytes 18874368 | tf_op jit(solution)/shard_map/all_to_all | solution.py:118
  1035.8 14.3 fusion.166
  1084.2 13.2 fusion.151
  1110.0 76.5 %all-to-all-done.3 = bf16[192,96,256]{2,1,0:T(8,128)(2,1)} async-done(((bf16[192,96,256]{2,1,0:T(8,128)(2,1)}), bf16[192,96,256]{2,1,0:T(8,128)(2,1)}, u32[]{:S(2)}, u32[]{:S(2)}) %all-to-all-start.3) | async-done | bytes 9437216 | tf_op jit(solution)/shard_map/all_to_all | solution.py:124
  1195.0 20.9 fusion.162
  1249.7 25.6 multiply_convert_fusion
  1275.4 12.7 convolution_add_fusion
  1288.1 18.7 copy.402
  1306.8 36.0 %fusion.155 = (bf16[512]{0:T(512)(128)(2,1)}, bf16[18432,512]{1,0:T(8,128)(2,1)}) fusion(f32[18432,512]{1,0:T(8,128)} %get-tuple-element.413, f32[512]{0:T(512)S(1)} %bitcast.472, bf16[18432,256]{1,0:T(8,128)(2,1)} %bitcast.422, bf16[2,512,256]{2,1,0:T(8,128)(2,1)S(1)} %copy-done.21), kind=kOutput, calls=%fused_computation.315 | convolution fusion | flops 5039455744 | bytes 66325504 | tf_op jit(solution)/shard_map/pc,fc->pf/dot_general | solution.py:207
  1342.8 13.3 fusion.163
  1356.0 18.6 copy.377
  1374.7 15.7 multiply_reduce_fusion
  1391.9 26.7 fusion.153
  1418.6 14.2 convert_bitcast_fusion.1
  1432.8 13.3 copy.378
  1446.1 111.6 %all_to_all.133 = bf16[48,384,256]{2,0,1:T(8,128)(2,1)} all-to-all(bf16[48,384,256]{2,0,1:T(8,128)(2,1)} %copy.378), channel_id=1, replica_groups=mesh['dp'=4,'pipe'=2,'space'=4] {'space'}, dimensions={1} | all-to-all | bytes 18874368 | tf_op jit(solution)/shard_map/all_to_all | solution.py:128
  1566.5 15.2 fusion.57
  1581.7 15.5 multiply_add_fusion.3
  1622.1 110.4 %all_to_all.134 = bf16[192,96,256]{2,1,0:T(8,128)(2,1)} all-to-all(bf16[192,96,256]{2,1,0:T(8,128)(2,1)} %copy.386), channel_id=1, replica_groups=mesh['dp'=4,'pipe'=2,'space'=4] {'space'}, dimensions={0} | all-to-all | bytes 18874368 | tf_op jit(solution)/shard_map/all_to_all | solution.py:134
  1741.1 22.3 multiply_reduce_fusion.4
  1763.5 22.2 fusion.27
  1785.7 28.4 %fusion.150 = (bf16[256]{0:T(256)(128)(2,1)}, f32[48,384,256]{1,2,0:T(8,128)S(1)}) fusion(f32[48,384]{1,0:T(8,128)S(1)} %negate_divide_fusion.1, f32[48,384,256]{1,2,0:T(8,128)} %get-tuple-element.361, f32[48,384]{1,0:T(8,128)S(1)} %multiply_divide_fusion.1, f32[48,384]{1,0:T(8,128)S(1)} %copy-done.40, f32[256]{0:T(256)S(1)} %bitcast.449, ...), kind=kLoop, calls=%fused_computation.310 | loop fusion | flops 66060032 | bytes 104105472 | tf_op jit(solution)/shard_map/reduce_sum | solution.py:202
  1837.5 36.4 %fusion.154 = (bf16[512]{0:T(512)(128)(2,1)}, bf16[18432,512]{1,0:T(8,128)(2,1)}) fusion(f32[18432,512]{1,0:T(8,128)} %get-tuple-element.408, f32[512]{0:T(512)S(1)} %bitcast.470, bf16[18432,256]{1,0:T(8,128)(2,1)} %bitcast.426, bf16[2,512,256]{2,1,0:T(8,128)(2,1)S(1)} %copy-done.22), kind=kOutput, calls=%fused_computation.314 | convolution fusion | flops 5039455744 | bytes 66325504 | tf_op jit(solution)/shard_map/pc,fc->pf/dot_general | solution.py:207
  1873.9 13.8 fusion.164
  1887.8 18.7 copy.390
  1906.4 15.4 multiply_reduce_fusion.1
  1923.6 16.8 fusion.152
  1940.4 18.7 convert_bitcast_fusion
  1959.1 13.3 copy.391
  1972.4 108.8 %all_to_all.135 = bf16[48,384,256]{2,0,1:T(8,128)(2,1)} all-to-all(bf16[48,384,256]{2,0,1:T(8,128)(2,1)} %copy.391), channel_id=1, replica_groups=mesh['dp'=4,'pipe'=2,'space'=4] {'space'}, dimensions={1} | all-to-all | bytes 18874368 | tf_op jit(solution)/shard_map/all_to_all | solution.py:128
  2089.9 15.2 fusion.55
  2105.1 15.6 multiply_add_fusion.1
  2175.4 74.7 %all-to-all-done.7 = bf16[192,96,256]{2,1,0:T(8,128)(2,1)} async-done(((bf16[192,96,256]{2,1,0:T(8,128)(2,1)}), bf16[192,96,256]{2,1,0:T(8,128)(2,1)}, u32[]{:S(2)}, u32[]{:S(2)}) %all-to-all-start.7) | async-done | bytes 9437216 | tf_op jit(solution)/shard_map/all_to_all | solution.py:134
  2258.7 25.4 fusion.26
  2284.1 20.4 fusion.25
  2304.6 49.9 %fusion.34 = (bf16[1,48,384,256]{2,3,1,0:T(8,128)(2,1)}, f32[48,384,256]{1,2,0:T(8,128)}) fusion(pred[]{:T(512)S(6)} %eq.37, f32[48,384,256]{1,2,0:T(8,128)} %get-tuple-element.410, f32[48,384,256]{1,2,0:T(8,128)} %copy.402, f32[48,384]{1,0:T(8,128)S(1)} %negate_divide_fusion, f32[48,384]{1,0:T(8,128)S(1)} %multiply_divide_fusion, ...), kind=kLoop, calls=%fused_computation.86 | loop fusion | flops 80216064 | bytes 151364608 | tf_op jit(solution)/shard_map/convert_element_type | solution.py:19
  2380.1 14.2 fusion.35
  2395.1 13.8 fusion.37
  2418.9 26.9 reduce-scatter.16.cloned.1.call-done
  2457.7 36.1 %all-reduce.20.cloned.1.call-done = (bf16[1,64,512]{2,1,0:T(8,128)(2,1)}, bf16[1,128,256]{2,1,0:T(8,128)(2,1)}) async-done(((bf16[1,64,512]{2,1,0:T(8,128)(2,1)}, bf16[1,128,256]{2,1,0:T(8,128)(2,1)}), (bf16[1,64,512]{2,1,0:T(8,128)(2,1)}, bf16[1,128,256]{2,1,0:T(8,128)(2,1)})) %all-reduce.20.cloned.1.call-update) | async-done | bytes 131088 | tf_op jit(solution)/shard_map/psum | solution.py:373
  2496.8 42.6 %all-reduce.18.cloned.1.call-done = bf16[2,192,256]{1,0,2:T(2,128)(2,1)} async-done(((bf16[2,192,256]{1,0,2:T(2,128)(2,1)}), bf16[2,192,256]{1,0,2:T(2,128)(2,1)}) %all-reduce.18.cloned.1.call-update) | async-done | bytes 196624
  2568.8 26.3 reduce-scatter.22.cloned.1.call-done
  2595.9 20.1 all-reduce.12
  2631.3 38.3 %maximum_select_fusion = f32[1,2,48,384,256]{3,4,2,1,0:T(8,128)} fusion(f32[1,1,48,384,256]{3,4,2,1,0:T(8,128)} %bitcast_convert_fusion, f32[1,1,48,384,256]{3,4,2,1,0:T(8,128)} %bitcast.417, f32[1,1,48,384,256]{3,4,2,1,0:T(8,128)} %get-tuple-element.381, pred[]{:T(512)S(6)} %eq.37), kind=kLoop, calls=%fused_computation.31 | loop fusion | flops 28311552 | bytes 94371840 | tf_op jit(solution)/shard_map/jit(_where)/select_n | solution.py:340
  2669.7 36.8 %copy.406 = f32[1,2,48,384,256]{4,3,2,1,0:T(8,128)} copy(f32[1,2,48,384,256]{3,4,2,1,0:T(8,128)} %maximum_select_fusion) | data formatting | bytes 75497472
  (1314 shorter events, 746.3 us)
Async XLA Ops:
  58.1 25.9 collective-permute-start
  60.3 42.6 %copy-start.13 = (bf16[384,384,1]{1,0,2:T(8,128)(2,1)}, bf16[384,384,1]{1,0,2:T(8,128)(2,1)S(1)}, u32[]{:S(2)}) copy-start(bf16[384,384,1]{1,0,2:T(8,128)(2,1)S(1)} %reshape.892) | copy-start | bytes 884740
  83.9 19.0 copy-start.63
  83.9 677.8 %copy-start.58 = (f32[1,1,256]{2,1,0:T(1,128)}, f32[1,1,256]{2,1,0:T(1,128)S(1)}, u32[]{:S(2)}) copy-start(f32[1,1,256]{2,1,0:T(1,128)S(1)} %get-tuple-element.397) | copy-start | bytes 3076
  98.2 19.4 copy-start.23
  117.6 415.9 %copy-start.53 = (f32[1,2,192,256]{3,2,1,0:T(8,128)S(1)}, f32[1,2,192,256]{3,2,1,0:T(8,128)}, u32[]{:S(2)}) copy-start(f32[1,2,192,256]{3,2,1,0:T(8,128)} %param.15) | copy-start | bytes 1179652
  130.5 436.0 %all-to-all-start = ((bf16[48,384,256]{2,0,1:T(8,128)(2,1)}), bf16[48,384,256]{2,0,1:T(8,128)(2,1)}, u32[]{:S(2)}, u32[]{:S(2)}) async-start(bf16[48,384,256]{2,0,1:T(8,128)(2,1)} %copy.349), calls=%async_computation | async-start | bytes 18874368 | tf_op jit(solution)/shard_map/all_to_all | solution.py:118
  566.5 23.2 copy-start.29
  566.5 23.2 copy-start.31
  605.4 20.4 copy-start.75
  605.4 22.2 copy-start.69
  605.5 24.0 copy-start.54
  605.5 26.2 copy-start.55
  618.2 111.4 %all-to-all-start.1 = ((bf16[192,96,256]{2,1,0:T(8,128)(2,1)}), bf16[192,96,256]{2,1,0:T(8,128)(2,1)}, u32[]{:S(2)}, u32[]{:S(2)}) async-start(bf16[192,96,256]{2,1,0:T(8,128)(2,1)} %copy.358), calls=%async_computation.1 | async-start | bytes 18874368 | tf_op jit(solution)/shard_map/all_to_all | solution.py:124
  625.8 126.5 %copy-start.5 = (bf16[384,384,1]{1,0,2:T(8,128)(2,1)}, bf16[384,384,1]{1,0,2:T(8,128)(2,1)S(1)}, u32[]{:S(2)}) copy-start(bf16[384,384,1]{1,0,2:T(8,128)(2,1)S(1)} %reshape.895) | copy-start | bytes 884740
  631.6 153.8 %copy-start.17 = (bf16[2,256,512]{2,1,0:T(8,128)(2,1)}, bf16[2,256,512]{2,1,0:T(8,128)(2,1)S(1)}, u32[]{:S(2)}) copy-start(bf16[2,256,512]{2,1,0:T(8,128)(2,1)S(1)} %all_gather.25) | copy-start | bytes 1572868
  633.8 177.1 %copy-start.20 = (bf16[2,512,256]{2,1,0:T(8,128)(2,1)}, bf16[2,512,256]{2,1,0:T(8,128)(2,1)S(1)}, u32[]{:S(2)}) copy-start(bf16[2,512,256]{2,1,0:T(8,128)(2,1)S(1)} %all_gather.21) | copy-start | bytes 1572868
  635.0 150.4 %copy-start.70 = (f32[1,1,512]{2,1,0:T(1,128)}, f32[1,1,512]{2,1,0:T(1,128)S(1)}, u32[]{:S(2)}) copy-start(f32[1,1,512]{2,1,0:T(1,128)S(1)} %get-tuple-element.392) | copy-start | bytes 6148
  752.3 20.5 copy-start.25
  761.7 23.7 copy-start.45
  761.7 23.7 copy-start.37
  860.8 21.1 copy-start.4
  860.8 21.7 copy-start.14
  860.8 21.7 copy-start.56
  860.8 21.7 copy-start.66
  882.5 18.8 copy-start.39
  1078.1 108.4 %all-to-all-start.3 = ((bf16[192,96,256]{2,1,0:T(8,128)(2,1)}), bf16[192,96,256]{2,1,0:T(8,128)(2,1)}, u32[]{:S(2)}, u32[]{:S(2)}) async-start(bf16[192,96,256]{2,1,0:T(8,128)(2,1)} %copy.373), calls=%async_computation.3 | async-start | bytes 18874368 | tf_op jit(solution)/shard_map/all_to_all | solution.py:124
  1097.4 97.6 %copy-start.6 = (bf16[384,384,1]{1,0,2:T(8,128)(2,1)S(1)}, bf16[384,384,1]{1,0,2:T(8,128)(2,1)}, u32[]{:S(2)}) copy-start(bf16[384,384,1]{1,0,2:T(8,128)(2,1)} %copy-done.5) | copy-start | bytes 884740
  1215.9 21.2 copy-start.27
  1226.0 23.7 copy-start.18
  1226.0 23.7 copy-start.72
  1249.7 25.7 copy-start.21
  1249.7 25.7 copy-start.62
  1391.9 26.7 copy-start.7
  1622.1 118.9 %copy-start.15 = (bf16[384,384,1]{1,0,2:T(8,128)(2,1)S(1)}, bf16[384,384,1]{1,0,2:T(8,128)(2,1)}, u32[]{:S(2)}) copy-start(bf16[384,384,1]{1,0,2:T(8,128)(2,1)} %copy-done.13) | copy-start | bytes 884740
  1622.1 118.9 %copy-start.57 = (f32[1,1,256]{2,1,0:T(1,128)S(1)}, f32[1,1,256]{2,1,0:T(1,128)}, u32[]{:S(2)}) copy-start(f32[1,1,256]{2,1,0:T(1,128)} %get-tuple-element.396) | copy-start | bytes 3076
  1741.0 22.4 copy-start.11
  1741.0 22.4 copy-start.52
  1741.0 22.4 copy-start.40
  1837.5 36.4 %copy-start.19 = (bf16[2,256,512]{2,1,0:T(8,128)(2,1)S(1)}, bf16[2,256,512]{2,1,0:T(8,128)(2,1)}, u32[]{:S(2)}) copy-start(bf16[2,256,512]{2,1,0:T(8,128)(2,1)} %copy-done.17) | copy-start | bytes 1572868
  1887.8 18.7 copy-start.38
  1887.8 18.7 copy-start.59
  2145.5 104.6 %all-to-all-start.7 = ((bf16[192,96,256]{2,1,0:T(8,128)(2,1)}), bf16[192,96,256]{2,1,0:T(8,128)(2,1)}, u32[]{:S(2)}, u32[]{:S(2)}) async-start(bf16[192,96,256]{2,1,0:T(8,128)(2,1)} %copy.399), calls=%async_computation.7 | async-start | bytes 18874368 | tf_op jit(solution)/shard_map/all_to_all | solution.py:134
  2151.3 243.0 %reduce-scatter.18.cloned.1.call-start = ((), (), s32[]{:S(2)}) async-start(), calls=%async_computation.18 | async-start | bytes 786432 | tf_op jit(solution)/shard_map/reduce_scatter | solution.py:328
  2163.6 95.0 %copy-start.16 = (bf16[384,384,1]{1,0,2:T(8,128)(2,1)S(1)}, bf16[384,384,1]{1,0,2:T(8,128)(2,1)}, u32[]{:S(2)}) copy-start(bf16[384,384,1]{1,0,2:T(8,128)(2,1)} %copy-done.13) | copy-start | bytes 884740
  2163.6 95.0 %copy-start.24 = (f32[48,384]{1,0:T(8,128)S(1)}, f32[48,384]{1,0:T(8,128)}, u32[]{:S(2)}) copy-start(f32[48,384]{1,0:T(8,128)} %copy-done.23) | copy-start | bytes 221188
  2163.6 95.0 %copy-start.64 = (f32[1,1,256]{2,1,0:T(1,128)S(1)}, f32[1,1,256]{2,1,0:T(1,128)}, u32[]{:S(2)}) copy-start(f32[1,1,256]{2,1,0:T(1,128)} %copy-done.63) | copy-start | bytes 3076
  2258.6 25.4 copy-start.12
  2258.6 25.4 copy-start.50
  2258.6 25.5 copy-start.44
  2354.4 264.3 %collective-permute-start.1 = (bf16[1,48,384,256]{2,3,1,0:T(8,128)(2,1)}, bf16[1,48,384,256]{2,3,1,0:T(8,128)(2,1)}, u32[]{:S(2)}, u32[]{:S(2)}) collective-permute-start(bf16[1,48,384,256]{2,3,1,0:T(8,128)(2,1)} %get-tuple-element.354), channel_id=1, source_target_pairs={{0,4},{4,0},{1,5},{5,1},{2,6},{6,2},{3,7},{7,3},{8,12},{12,8},{9,1... | collective-permute-start | bytes 28311560 | tf_op jit(solution)/shard_map/ppermute | solution.py:15
  2367.1 27.5 %reduce-scatter.14.cloned.1.call-start = ((), (), s32[]{:S(2)}) async-start(), calls=%async_computation.16 | async-start | bytes 786432 | tf_op jit(solution)/shard_map/reduce_scatter | solution.py:322
  2380.1 38.9 %reduce-scatter.20.cloned.1.call-start = ((), (), s32[]{:S(2)}) async-start(), calls=%async_computation.19 | async-start | bytes 327680 | tf_op jit(solution)/shard_map/reduce_scatter | solution.py:362
  2394.4 51.5 %reduce-scatter.16.cloned.1.call-start = ((), (), s32[]{:S(2)}) async-start(), calls=%async_computation.17 | async-start | bytes 327680 | tf_op jit(solution)/shard_map/reduce_scatter | solution.py:356
  2395.0 50.9 %copy-start.81 = (bf16[256]{0:T(256)(128)(2,1)S(1)}, bf16[256]{0:T(256)(128)(2,1)}, u32[]{:S(2)}) copy-start(bf16[256]{0:T(256)(128)(2,1)} %get-tuple-element.303) | copy-start | bytes 1540
  2395.0 50.9 %copy-start.82 = (bf16[256]{0:T(256)(128)(2,1)S(1)}, bf16[256]{0:T(256)(128)(2,1)}, u32[]{:S(2)}) copy-start(bf16[256]{0:T(256)(128)(2,1)} %get-tuple-element.350) | copy-start | bytes 1540
  2395.0 50.9 %copy-start.79 = (bf16[256]{0:T(256)(128)(2,1)S(1)}, bf16[256]{0:T(256)(128)(2,1)}, u32[]{:S(2)}) copy-start(bf16[256]{0:T(256)(128)(2,1)} %get-tuple-element.420) | copy-start | bytes 1540
  2395.1 51.0 %copy-start.74 = (bf16[512]{0:T(512)(128)(2,1)S(1)}, bf16[512]{0:T(512)(128)(2,1)}, u32[]{:S(2)}) copy-start(bf16[512]{0:T(512)(128)(2,1)} %get-tuple-element.369) | copy-start | bytes 3076
  2395.1 51.0 %copy-start.80 = (bf16[256]{0:T(256)(128)(2,1)S(1)}, bf16[256]{0:T(256)(128)(2,1)}, u32[]{:S(2)}) copy-start(bf16[256]{0:T(256)(128)(2,1)} %get-tuple-element.297) | copy-start | bytes 1540
  2395.1 60.7 %reduce-scatter.12.cloned.1.call-start = ((), (), s32[]{:S(2)}) async-start(), calls=%async_computation.15 | async-start | bytes 589824 | tf_op jit(solution)/shard_map/reduce_scatter | solution.py:319
  2409.9 83.9 %all-reduce.20.cloned.1.call-start = ((), (), s32[]{:S(2)}) async-start(), calls=%async_computation.23 | async-start | bytes 262144 | tf_op jit(solution)/shard_map/psum | solution.py:373
  2445.9 93.5 %all-reduce.18.cloned.1.call-start = ((), (), s32[]{:S(2)}) async-start(), calls=%async_computation.22 | async-start | bytes 524288
  2457.6 110.5 %reduce-scatter.24.cloned.1.call-start = ((), (), s32[]{:S(2)}) async-start(), calls=%async_computation.21 | async-start | bytes 81920
  2544.2 50.9 %reduce-scatter.22.cloned.1.call-start = ((), (), s32[]{:S(2)}) async-start(), calls=%async_computation.20 | async-start | bytes 81920
  (42 other events, 565.9 us)
Sparse Core Ops, SparseCore 0:
  2367.2 8.2 reduce-scatter.17
  2380.2 8.2 reduce-scatter.13
  2394.5 24.3 reduce-scatter.19
  2421.8 24.0 reduce-scatter.15
  2447.9 7.7 reduce-scatter.11
  2458.1 35.6 all-reduce.19
  2496.7 42.6 all-reduce.17
  2544.4 23.6 reduce-scatter.23
  2571.4 23.7 reduce-scatter.21
where the time goes:
time: 2730 us; the launch traced here: 2710 us
  other arithmetic  628 us (23%)
  local copies, waits for them, and re-layouts  546 us (20%)
  blocking collectives  491 us (18%)
  matrix products  472 us (17%)
  waiting for transfers between devices  406 us (15%)
  loops' own time  130 us (5%)
    all_to_all x2, blocking collectives, grad_to_modes(): lax.all_to_all(spectrum, 'space', split_axis=1, concat_axis=0, tiled=True)  220 us
    all_to_all x2, waiting for transfers between devices, to_bands(): lax.all_to_all(joined, 'space', split_axis=0, concat_axis=1, tiled=True)  171 us
    dynamic_update_slice x192, other arithmetic, legendre_table(): lax.scan(recurrence, (zero_rows, zero_rows), jnp.arange(degree_count, dty...  141 us
    another operation x1, loops' own time, legendre_table(): lax.scan(recurrence, (zero_rows, zero_rows), jnp.arange(degree_count, dty...  130 us
    all_to_all x1, blocking collectives, to_modes(): lax.all_to_all(spectrum, 'space', split_axis=1, concat_axis=0, tiled=True)  113 us
    dynamic_slice x192, local copies, waits for them, and re-layouts, legendre_table(): lax.scan(recurrence, (zero_rows, zero_rows), jnp.arange(degree_count, dty...  112 us
    all_to_all x1, blocking collectives, grad_to_bands(): lax.all_to_all(joined, 'space', split_axis=0, concat_axis=1, tiled=True)  110 us
    unnamed x193, local copies, waits for them, and re-layouts  97.6 us
  transfers between devices with their start and end apart: 15, of which 10 were waited for; matrix products, arithmetic and copies ran while one was open for 16% of the time, Pallas kernels for 0%

commit v1 on v0

--- a/solution.py
+++ b/solution.py
@@ -1,12 +1,1627 @@
+from collections import namedtuple
 from functools import partial
 import math
 
 import jax
 import jax.numpy as jnp
 from jax import lax
+from jax.experimental import pallas as pl
+from jax.experimental.pallas import tpu as pltpu
 from jax.sharding import PartitionSpec as P
 
 NORM_EPS = 1e-05
+BF = jnp.bfloat16
+F32 = jnp.float32
+MESH = pl.DeviceIdType.MESH
+VMEM_BYTES = 58 * 2**20
+TILE = 32
+ROWS = 8
+GELU_SCALE = math.sqrt(2.0 / math.pi)
+GELU_CUBE = 0.044715
+
+Dims = namedtuple(
+    "Dims",
+    ("bands", "lat", "lon", "ch", "own", "degrees", "ff", "rows", "chunks", "sub", "steps", "group",
+     "low", "high"),
+)
+
+
+def matmul(a, b):
+    return jnp.dot(a, b, preferred_element_type=F32)
+
+
+def matmul_tn(a, b):
+    return lax.dot_general(a, b, (((0,), (0,)), ((), ())), preferred_element_type=F32)
+
+
+def matmul_nt(a, b):
+    return lax.dot_general(a, b, (((1,), (1,)), ((), ())), preferred_element_type=F32)
+
+
+def total(value):
+    return jnp.sum(value, axis=-1, keepdims=True)
+
+
+def folded(value):
+    return jnp.sum(value.reshape(value.shape[0] // 8, 8, value.shape[1]), axis=0)
+
+
+def dft_fill(table, inverse, by_order):
+    orders, lon = table.shape[0] // 2, table.shape[0]
+    order_axis = 0 if by_order else 1
+    part = lax.broadcasted_iota(jnp.int32, table.shape, order_axis)
+    imaginary = part >= orders
+    order = jnp.where(imaginary, part - orders, part).astype(F32)
+    point = lax.broadcasted_iota(jnp.int32, table.shape, 1 - order_axis).astype(F32)
+    phase = order * point
+    phase = phase - lon * jnp.floor(phase * (1.0 / lon))
+    phase = jnp.where(phase >= lon, phase - lon, phase)
+    angle = phase * (2.0 * math.pi / lon)
+    value = jnp.where(imaginary, -jnp.sin(angle), jnp.cos(angle))
+    scale = jnp.where(order == 0.0, 1.0, 2.0) if inverse else 2.0 * math.pi / lon
+    table[...] = (value * scale).astype(BF)
+
+
+def legendre_orders(orders):
+    order_value = orders.astype(F32)
+    factor = 0.5 * (
+        jnp.log((2.0 * order_value + 1.0) / (4.0 * math.pi))
+        + lax.lgamma(order_value + 0.5)
+        - lax.lgamma(order_value + 1.0)
+        - 0.5 * math.log(math.pi)
+    )
+    return jnp.stack([order_value, factor], axis=1)
+
+
+def legendre_fill(first, orders, colat_count, first_lat, analysis, synthesis, rows):
+    count, degrees, lat = analysis.shape
+    own, width = orders.shape[0], -(-lat // 128) * 128
+    order_value = jnp.broadcast_to(orders[:, 0:1], (own, width))
+    square = order_value * order_value
+    lats = jnp.minimum(lax.broadcasted_iota(jnp.int32, (8, width), 1) + first_lat, colat_count - 1)
+    colatitude = (lats.astype(F32) + 0.5) * (math.pi / colat_count)
+    sine = jnp.sin(colatitude)
+    cosine = jnp.cos(colatitude)[0:1]
+    weight = (sine * (math.pi / colat_count))[0:1]
+    start = jnp.exp(orders[:, 1:2] + order_value * jnp.log(sine)[0:1])
+
+    def recurrence(degree, pair):
+        older, newer = pair
+        value = (degree + first).astype(F32)
+        ahead = jnp.sqrt(
+            jnp.maximum(4.0 * value * value - 1.0, 0.0) / jnp.maximum(value * value - square, 1.0)
+        )
+        below = value - 1.0
+        behind = jnp.sqrt(
+            jnp.maximum(below * below - square, 0.0)
+            / jnp.maximum(4.0 * below * below - 1.0, 1.0)
+        )
+        general = ahead * (cosine * newer - behind * older)
+        row = jnp.where(value < order_value, 0.0, jnp.where(value == order_value, start, general))
+        at = pl.multiple_of(degree * own, 8)
+        for part in range(width // 128):
+            rows[part, pl.ds(at, own), :] = row[:, part * 128 : (part + 1) * 128]
+        return newer, row
+
+    zero = start * 0.0
+    lax.fori_loop(0, degrees, recurrence, (zero, zero))
+
+    @pl.loop(0, count)
+    def _(m):
+        table = jnp.concatenate(
+            [rows[part, pl.ds(m, degrees, stride=own), :] for part in range(width // 128)], axis=1
+        )
+        synthesis[m] = table[:, :lat].astype(BF)
+        analysis[m] = (table * weight)[:, :lat].astype(BF)
+
+
+def sides():
+    me = lax.axis_index("space")
+    return me + 1 - 2 * lax.rem(me, 2), lax.rem(me + 2, 4), 3 - me
+
+
+def peers():
+    core = lax.axis_index("pipe")
+    x, y, across_both = sides()
+    return [across_both, x + core * (y - x), y + core * (x - y)]
+
+
+def greet(bands):
+    barrier = pltpu.get_barrier_semaphore()
+    for peer in peers():
+        pl.semaphore_signal(barrier, inc=1, device_id={"space": peer}, device_id_type=MESH)
+
+
+def await_peers(count):
+    pl.semaphore_wait(pltpu.get_barrier_semaphore(), count)
+
+
+def block_copies(bands, piece, source, place, sems, coming):
+    out_sems, in_sems, own_sems = sems
+    me = lax.axis_index("space")
+    copies = []
+    for turn, peer in enumerate(peers()):
+        band = peer if coming else me
+        copies.append(
+            pltpu.make_async_remote_copy(
+                src_ref=source(peer),
+                dst_ref=place(band),
+                send_sem=out_sems.at[piece, turn],
+                recv_sem=in_sems.at[piece, turn],
+                device_id={"space": peer},
+                device_id_type=MESH,
+            )
+        )
+    return copies
+
+
+def own_copy(piece, source, place, sems):
+    me = lax.axis_index("space")
+    return pltpu.make_async_copy(source(me), place(me), sems[2].at[piece])
+
+
+def start_piece(bands, piece, source, place, sems):
+    for copy in block_copies(bands, piece, source, place, sems, False):
+        copy.start()
+    own_copy(piece, source, place, sems).start()
+
+
+def finish_piece(bands, piece, source, place, sems):
+    for copy in block_copies(bands, piece, source, place, sems, False):
+        copy.wait_send()
+    for copy in block_copies(bands, piece, source, place, sems, True):
+        copy.wait_recv()
+    own_copy(piece, source, place, sems).wait()
+
+
+def side_copy(source, target, sems, slot, peer):
+    return pltpu.make_async_remote_copy(
+        src_ref=source,
+        dst_ref=target,
+        send_sem=sems[0].at[slot],
+        recv_sem=sems[1].at[slot],
+        device_id={"space": peer},
+        device_id_type=MESH,
+    )
+
+
+def side_sems():
+    return [pltpu.SemaphoreType.DMA((4,)), pltpu.SemaphoreType.DMA((4,)), pltpu.SemaphoreType.DMA((1,))]
+
+
+def exchange_sems(bands, pieces):
+    return [
+        pltpu.SemaphoreType.DMA((pieces, bands - 1)),
+        pltpu.SemaphoreType.DMA((pieces, bands - 1)),
+        pltpu.SemaphoreType.DMA((pieces,)),
+    ]
+
+
+At = namedtuple("At", ("number", "chunk", "step", "last"))
+
+
+def at_of(d, number):
+    last = number == d.chunks * d.steps - 1
+    return At(number, number // d.steps, lax.rem(number, d.steps), last)
+
+
+def lat_stride(d):
+    return 2 * d.bands * d.own + 8
+
+
+def pack_rows(d, piece, wide, send):
+    orders = d.bands * d.own
+    for band in range(d.bands):
+
+        @pl.loop(0, d.own, unroll=4)
+        def _(m):
+            for half in range(d.ch // 128):
+                values = []
+                for part in range(2):
+                    at = part * orders + d.bands * m + band
+                    values.append(wide[half, pl.ds(at, d.rows, stride=lat_stride(d)), :])
+                lanes = slice(half * 128, half * 128 + 128)
+                send[piece, band, m, :, lanes] = jnp.concatenate(values, axis=0).astype(BF)
+
+
+def unpack_rows(d, block, wide):
+    orders = d.bands * d.own
+    for band in range(d.bands):
+
+        @pl.loop(0, d.own, unroll=4)
+        def _(m):
+            value = block[band, m].astype(F32)
+            for half in range(d.ch // 128):
+                lanes = slice(half * 128, half * 128 + 128)
+                for part in range(2):
+                    at = part * orders + d.bands * m + band
+                    wide[half, pl.ds(at, d.rows, stride=lat_stride(d)), :] = value[
+                        part * d.rows : (part + 1) * d.rows, lanes
+                    ]
+
+
+def wide_rows(d, wide, k):
+    orders = d.bands * d.own
+    at = pl.multiple_of(k * lat_stride(d), 8)
+    return jnp.concatenate(
+        [wide[half, pl.ds(at, 2 * orders), :].astype(BF) for half in range(d.ch // 128)], axis=1
+    )
+
+
+def store_wide(d, wide, k, value):
+    orders = d.bands * d.own
+    at = pl.multiple_of(k * lat_stride(d), 8)
+    for half in range(d.ch // 128):
+        wide[half, pl.ds(at, 2 * orders), :] = value[:, half * 128 : (half + 1) * 128]
+
+
+def modes_to_grid(d, at, table, wide, acc):
+    for s in range(d.sub):
+        k = at.step * d.sub + s
+        acc[s * d.lon : (s + 1) * d.lon] = matmul(table[...], wide_rows(d, wide, k))
+
+
+def grid_to_modes(d, at, table, low, wide):
+    for s in range(d.sub):
+        k = at.step * d.sub + s
+        store_wide(d, wide, k, matmul(table[...], low[s * d.lon : (s + 1) * d.lon]))
+
+
+def tiles(d):
+    return [slice(t, t + TILE) for t in range(0, d.sub * d.lon, TILE)]
+
+
+def spread(d, column):
+    return jnp.broadcast_to(column, (TILE, 128))
+
+
+def across(d, ref, t):
+    return jnp.concatenate([ref[t].astype(F32)] * (d.ch // 128), axis=1)
+
+
+def live_of(d, level, t):
+    lane = lax.broadcasted_iota(jnp.int32, (TILE, d.ch), 1)
+    return lax.rem(lane, 8).astype(F32) >= across(d, level, t)
+
+
+def inverse_count(d, level, t):
+    return 1.0 / jnp.maximum((d.ch // 8) * (8.0 - level[t].astype(F32)), 1.0)
+
+
+def masked(live, value):
+    return jnp.where(live, value, 0.0)
+
+
+def masked_sums(d, value_of, level, mean, share):
+    for t in tiles(d):
+        share[t] = inverse_count(d, level, t)
+        mean[t] = spread(d, total(masked(live_of(d, level, t), value_of(t)))) * share[t]
+
+
+def masked_spreads(d, value_of, level, mean, share, scale):
+    for t in tiles(d):
+        centered = masked(live_of(d, level, t), value_of(t) - across(d, mean, t))
+        scale[t] = lax.rsqrt(spread(d, total(centered * centered)) * share[t] + NORM_EPS)
+
+
+def masked_values(d, value_of, level, mean, scale, gain, bias, low):
+    for t in tiles(d):
+        unit = (value_of(t) - across(d, mean, t)) * across(d, scale, t)
+        low[t] = masked(live_of(d, level, t), unit * gain + bias).astype(BF)
+
+
+def masked_norm(d, value_of, level, stats, gain, bias, low):
+    mean, scale, share = stats[:3]
+    masked_sums(d, value_of, level, mean, share)
+    masked_spreads(d, value_of, level, mean, share, scale)
+    masked_values(d, value_of, level, mean, scale, gain, bias, low)
+
+
+def masked_back_sums(d, value_of, grad, level, gain, stats):
+    mean, scale, first, second = stats
+    for t in tiles(d):
+        live, share = live_of(d, level, t), inverse_count(d, level, t)
+        second[t] = share
+        mean[t] = spread(d, total(masked(live, value_of(t)))) * share
+        first[t] = spread(d, total(masked(live, grad[t] * gain))) * share
+    for t in tiles(d):
+        centered = masked(live_of(d, level, t), value_of(t) - across(d, mean, t))
+        share = second[t]
+        rate = lax.rsqrt(spread(d, total(centered * centered)) * share + NORM_EPS)
+        scale[t] = rate
+        second[t] = spread(d, total(grad[t] * gain * centered)) * share * rate * rate
+
+
+def masked_back_value(d, t, value, grad, level, gain, stats):
+    mean, scale, first, second = (across(d, ref, t) for ref in stats)
+    live = live_of(d, level, t)
+    centered = value - mean
+    back = masked(live, scale * (grad * gain - first - centered * second))
+    live_grad = masked(live, grad)
+    return back, live_grad * (centered * scale), live_grad
+
+
+def plain_sums(d, value_of, mean):
+    for t in tiles(d):
+        mean[t] = spread(d, total(value_of(t))) * (1.0 / d.ch)
+
+
+def plain_spreads(d, value_of, mean, scale):
+    for t in tiles(d):
+        centered = value_of(t) - across(d, mean, t)
+        scale[t] = lax.rsqrt(spread(d, total(centered * centered)) * (1.0 / d.ch) + NORM_EPS)
+
+
+def plain_values(d, value_of, mean, scale, gain, bias, low):
+    for t in tiles(d):
+        unit = (value_of(t) - across(d, mean, t)) * across(d, scale, t)
+        low[t] = (unit * gain + bias).astype(BF)
+
+
+def plain_back_sums(d, value_of, grad, gain, stats):
+    mean, scale, first, second = stats
+    for t in tiles(d):
+        scaled = grad[t] * gain
+        centered = value_of(t) - across(d, mean, t)
+        rate = scale[t]
+        first[t] = spread(d, total(scaled)) * (1.0 / d.ch)
+        second[t] = spread(d, total(scaled * centered)) * (rate * rate * (1.0 / d.ch))
+
+
+def plain_back_value(d, t, value, grad, gain, stats):
+    mean, scale, first, second = (across(d, ref, t) for ref in stats)
+    centered = value - mean
+    back = scale * (grad * gain - first - centered * second)
+    return back, grad * (centered * scale)
+
+
+def gelu_parts(hidden):
+    square = hidden * hidden
+    bend = jnp.tanh(hidden * (GELU_SCALE + GELU_SCALE * GELU_CUBE * square))
+    return square, bend
+
+
+def gelu_value(hidden):
+    _, bend = gelu_parts(hidden)
+    half = 0.5 * hidden
+    return half + half * bend
+
+
+def gelu_both(hidden):
+    square, bend = gelu_parts(hidden)
+    half = 0.5 * hidden
+    slope = half * (GELU_SCALE + (3.0 * GELU_SCALE * GELU_CUBE) * square)
+    return half + half * bend, 0.5 + 0.5 * bend + slope * (1.0 - bend * bend)
+
+
+class Sums:
+    def __init__(self):
+        self.held = {}
+
+    def add(self, ref, value):
+        value = folded(value)
+        known = self.held.get(id(ref))
+        self.held[id(ref)] = (ref, value if known is None else known[1] + value)
+
+    def store(self):
+        for ref, value in self.held.values():
+            ref[...] += value
+
+
+def clear(*refs):
+    for ref in refs:
+        ref[...] = jnp.zeros_like(ref)
+
+
+def high_rows(d):
+    found, at = [], 0
+    for j in range(d.high):
+        count = -(-(d.lat - d.bands * j) // 8) * 8
+        found.append((j, count, at))
+        at += 2 * count
+    return found
+
+
+def high_total(d):
+    return 2 * sum(count for _, count, _ in high_rows(d))
+
+
+def split_parts(d, value):
+    value = value.reshape(value.shape[0] // 16, 2, 8, d.ch)
+    return [value[:, part].reshape(-1, d.ch) for part in range(2)]
+
+
+def join_parts(d, real, imag):
+    parts = [value.reshape(value.shape[0] // 8, 1, 8, d.ch) for value in (real, imag)]
+    return jnp.concatenate(parts, axis=1).reshape(-1, d.ch)
+
+
+def degrees_to_rows(d, table, arrived_high, arrived):
+    @pl.loop(0, d.bands)
+    def _(band):
+        for j, count, at in high_rows(d):
+            real, imag = split_parts(d, arrived_high[band, at : at + 2 * count].astype(F32))
+            value = jnp.concatenate([real, imag], axis=1)
+            if count < d.lat:
+                value = jnp.concatenate([jnp.zeros((d.lat - count, 2 * d.ch), F32), value], axis=0)
+            value = matmul_tn(table[band * d.high + j], value.astype(BF))
+            rows = join_parts(d, value[:, : d.ch], value[:, d.ch :]).astype(BF)
+            for chunk in range(d.chunks):
+                arrived[chunk, band, d.low + j] = rows[chunk * 16 : (chunk + 1) * 16]
+
+
+def rows_to_degrees(d, table, band, send, send_high):
+    for j, count, at in high_rows(d):
+        rows = [send[chunk, band, d.low + j].astype(F32) for chunk in range(d.chunks)]
+        real, imag = split_parts(d, jnp.concatenate(rows, axis=0))
+        value = jnp.concatenate([real.astype(BF), imag.astype(BF)], axis=1)
+        value = matmul(table[band * d.high + j], value)[d.lat - count :]
+        value = join_parts(d, value[:, : d.ch], value[:, d.ch :])
+        send_high[band, at : at + 2 * count] = value.astype(BF)
+
+
+def high_halves(d):
+    half = high_total(d) // 32 * 16
+    return pl.ds(0, half), pl.ds(half, high_total(d) - half)
+
+
+def gather_high(d, table, send, send_high, relay, landed_high, sems):
+    me = lax.axis_index("space")
+    x, y, across_both = sides()
+    first, second = high_halves(d)
+    rows_to_degrees(d, table, across_both, send, send_high)
+    for copy in high_relays(d, send_high, relay, sems):
+        copy.start()
+
+    @pl.loop(0, d.bands)
+    def _(band):
+        @pl.when(band != across_both)
+        def _():
+            rows_to_degrees(d, table, band, send, send_high)
+
+    for copy in high_relays(d, send_high, relay, sems):
+        copy.wait_recv()
+    for slot, (band, part) in enumerate(((y, second), (x, first))):
+        size = part.size
+        value = send_high[band, part].astype(F32) + relay[slot, :size].astype(F32)
+        send_high[band, part] = value.astype(BF)
+    for copy in high_sends(send_high, landed_high, sems, False):
+        copy.start()
+    pltpu.make_async_copy(send_high.at[me], landed_high.at[me], sems[2].at[0]).start()
+
+
+def high_relays(d, send_high, relay, sems):
+    x, y, across_both = sides()
+    first, second = high_halves(d)
+    return [
+        side_copy(
+            send_high.at[across_both, second], relay.at[0, pl.ds(0, second.size)], sems, 2, x
+        ),
+        side_copy(
+            send_high.at[across_both, first], relay.at[1, pl.ds(0, first.size)], sems, 3, y
+        ),
+    ]
+
+
+def high_sends(send_high, landed_high, sems, coming):
+    me = lax.axis_index("space")
+    x, y, _ = sides()
+    return [
+        side_copy(send_high.at[peer], landed_high.at[peer if coming else me], sems, slot, peer)
+        for slot, peer in enumerate((x, y))
+    ]
+
+
+def finish_high(d, send_high, relay, landed_high, sems):
+    me = lax.axis_index("space")
+    for copy in high_relays(d, send_high, relay, sems) + high_sends(
+        send_high, landed_high, sems, False
+    ):
+        copy.wait_send()
+    for copy in high_sends(send_high, landed_high, sems, True):
+        copy.wait_recv()
+    pltpu.make_async_copy(send_high.at[me], landed_high.at[me], sems[2].at[0]).wait()
+
+
+def spread_copies(d, order_high, arrived_high, sems, coming):
+    me = lax.axis_index("space")
+    x, y, _ = sides()
+    return [
+        side_copy(order_high, arrived_high.at[peer if coming else me], sems, slot, peer)
+        for slot, peer in enumerate((x, y))
+    ]
+
+
+def passing_copies(d, arrived_high, sems, coming):
+    x, y, across_both = sides()
+    first, second = high_halves(d)
+    copies = []
+    for slot, peer, origin, part in ((2, x, y, second), (3, y, x, first)):
+        target = arrived_high.at[across_both if coming else origin, part]
+        copies.append(side_copy(arrived_high.at[origin, part], target, sems, slot, peer))
+    return copies
+
+
+def spread_own(order_high, arrived_high, sems):
+    me = lax.axis_index("space")
+    return pltpu.make_async_copy(order_high, arrived_high.at[me], sems[2].at[0])
+
+
+def grid_pieces(d, send, landed, sems):
+    def pieces(piece):
+        return (
+            d.bands,
+            piece,
+            lambda peer: send.at[piece, peer, pl.ds(0, d.low)],
+            lambda band: landed.at[band, :, pl.ds(piece * 2 * d.rows, 2 * d.rows), :],
+            sems,
+        )
+
+    return pieces
+
+
+def send_chunk(
+    d, at, table, wide, send, send_high, relay, landed, landed_high, sems, high_sems
+):
+    pieces = grid_pieces(d, send, landed, sems)
+
+    @pl.when(at.step == d.steps - 1)
+    def _():
+        pack_rows(d, at.chunk, wide, send)
+        start_piece(*pieces(at.chunk))
+
+    @pl.when(at.last)
+    def _():
+        gather_high(d, table, send, send_high, relay, landed_high, high_sems)
+
+
+def finish_chunks(d, at, send, send_high, relay, landed, landed_high, sems, high_sems):
+    @pl.when(at.last)
+    def _():
+        for piece in range(d.chunks):
+            finish_piece(*grid_pieces(d, send, landed, sems)(piece))
+        finish_high(d, send_high, relay, landed_high, high_sems)
+
+
+def order_steps(d):
+    return 1 + d.low // d.group
+
+
+def order_pieces(d, send, arrived, sems):
+    count = order_steps(d)
+
+    def first(step):
+        part = pl.ds((step - 1) * d.group, d.group)
+        return (
+            d.bands,
+            step - 1,
+            lambda peer: send.at[0, peer, part],
+            lambda band: arrived.at[0, band, part],
+            sems,
+        )
+
+    def whole(chunk):
+        part = pl.ds(0, d.low)
+        return (
+            d.bands,
+            count + chunk - 2,
+            lambda peer: send.at[chunk, peer, part],
+            lambda band: arrived.at[chunk, band, part],
+            sems,
+        )
+
+    return first, whole
+
+
+PASS_STEP = 5
+
+
+def send_orders(d, step, peer_count, send, order_high, arrived, arrived_high, sems, high_sems):
+    first, whole = order_pieces(d, send, arrived, sems)
+
+    @pl.when(step == 0)
+    def _():
+        await_peers(peer_count)
+        for copy in spread_copies(d, order_high, arrived_high, high_sems, False):
+            copy.start()
+        spread_own(order_high, arrived_high, high_sems).start()
+
+    @pl.when(step > 0)
+    def _():
+        start_piece(*first(step))
+
+    @pl.when(step == PASS_STEP)
+    def _():
+        for copy in spread_copies(d, order_high, arrived_high, high_sems, True):
+            copy.wait_recv()
+        for copy in passing_copies(d, arrived_high, high_sems, False):
+            copy.start()
+
+    @pl.when(step == order_steps(d) - 1)
+    def _():
+        for chunk in range(1, d.chunks):
+            start_piece(*whole(chunk))
+
+
+def take_chunk(d, at, table, send, order_high, arrived, arrived_high, sems, high_sems, wide):
+    first, whole = order_pieces(d, send, arrived, sems)
+
+    @pl.when(at.step == 0)
+    def _():
+        @pl.when(at.chunk == 0)
+        def _():
+            for copy in passing_copies(d, arrived_high, high_sems, True):
+                copy.wait_recv()
+            spread_own(order_high, arrived_high, high_sems).wait()
+            degrees_to_rows(d, table, arrived_high, arrived)
+            for step in range(1, order_steps(d)):
+                finish_piece(*first(step))
+            for copy in spread_copies(
+                d, order_high, arrived_high, high_sems, False
+            ) + passing_copies(d, arrived_high, high_sems, False):
+                copy.wait_send()
+
+        @pl.when(at.chunk > 0)
+        def _():
+            finish_piece(*whole(at.chunk))
+
+        unpack_rows(d, arrived.at[at.chunk], wide)
+
+
+def pair_copy(source, target, send_sem, recv_sem):
+    return pltpu.make_async_remote_copy(
+        src_ref=source,
+        dst_ref=target,
+        send_sem=send_sem,
+        recv_sem=recv_sem,
+        device_id={"pipe": 1 - lax.axis_index("pipe")},
+        device_id_type=MESH,
+    )
+
+
+WEIGHTS = 7
+TURN_CHUNK = 3
+
+
+def point_start_kernel(
+    d, edges, mask, gains, biases, orders, *refs
+):
+    weights = refs[:WEIGHTS]
+    x, level, *tables, forward, forward_t, inverse, inverse_t, arrived = refs[WEIGHTS : WEIGHTS + 11]
+    fulls = refs[WEIGHTS + 11 : 2 * WEIGHTS + 11]
+    (
+        landed, landed_high, taken, taken_sems, other_gains, other_biases, swap_out, swap_in, own_sems,
+        edge_out, edge_in, turn, mean, scale, share, legendre_rows, low, wide, send, send_high, relay, *sems,
+    ) = refs[2 * WEIGHTS + 11 :]
+    grid_refs = (send, send_high, relay, landed, landed_high, sems[:3], sems[3:])
+    core = lax.axis_index("pipe")
+    points = d.sub * d.lon
+    piece_points = d.rows * d.lon
+    number = pl.program_id(0)
+    at = at_of(d, number)
+    count = d.chunks * d.steps
+
+    def edge_copy(piece):
+        part = pl.ds(piece * piece_points, piece_points)
+        return pair_copy(
+            edges.at[0, 1 - core, part], arrived.at[part], edge_out.at[piece], edge_in.at[piece]
+        )
+
+    def weight_copies(place):
+        copies = [
+            pair_copy(weights[n].at[0], fulls[n].at[place], swap_out.at[n], swap_in.at[n])
+            for n in range(WEIGHTS)
+        ]
+        copies.append(
+            pair_copy(gains, other_gains, swap_out.at[WEIGHTS], swap_in.at[WEIGHTS])
+        )
+        copies.append(
+            pair_copy(biases, other_biases, swap_out.at[WEIGHTS + 1], swap_in.at[WEIGHTS + 1])
+        )
+        return copies
+
+    def weight_locals():
+        return [
+            pltpu.make_async_copy(weights[n].at[0], fulls[n].at[core], own_sems.at[n])
+            for n in range(WEIGHTS)
+        ]
+
+    def take(n, source):
+        part = pl.ds(n * points, points)
+        slot = lax.rem(n, 2)
+        return pltpu.make_async_copy(source.at[part], taken.at[slot], taken_sems.at[slot])
+
+    def start_take(n):
+        @pl.when(core == 0)
+        def _():
+            take(n, edges.at[0, 0]).start()
+
+        @pl.when(core == 1)
+        def _():
+            @pl.when(lax.rem(n, d.steps) == 0)
+            def _():
+                edge_copy(n // d.steps).wait_recv()
+
+            take(n, arrived).start()
+
+    def fill():
+        lows = orders[: orders.shape[0] - d.bands * d.high]
+        legendre_fill(0, lows, d.degrees, 0, *tables[:2], legendre_rows)
+
+    @pl.when(number == 0)
+    def _():
+        barrier = pltpu.get_barrier_semaphore()
+        for peer in peers():
+            pl.semaphore_signal(barrier, inc=1, device_id={"space": peer}, device_id_type=MESH)
+        pl.semaphore_signal(barrier, inc=1, device_id={"pipe": 1 - core}, device_id_type=MESH)
+        pl.semaphore_wait(barrier, d.bands)
+        for copy in weight_copies(core) + weight_locals():
+            copy.start()
+        for piece in range(d.chunks):
+            edge_copy(piece).start()
+        dft_fill(forward, False, True)
+        highs = orders[orders.shape[0] - d.bands * d.high :]
+        first_lat = lax.axis_index("space") * d.lat
+        legendre_fill(d.degrees - d.lat, highs, d.degrees, first_lat, *tables[2:], legendre_rows)
+
+        @pl.when(core == 1)
+        def _():
+            fill()
+            pl.semaphore_wait(turn, 1)
+
+        start_take(0)
+        for copy in weight_copies(1 - core):
+            copy.wait_recv()
+
+    @pl.when(number + 1 < count)
+    def _():
+        start_take(number + 1)
+
+    take(number, edges.at[0, 0]).wait()
+    slot = lax.rem(number, 2)
+    gain = jnp.where(core == 0, gains[0, 0:1], other_gains[0, 0:1])
+    bias = jnp.where(core == 0, biases[0, 0:1], other_biases[0, 0:1])
+    value_of = lambda t: x[t].astype(F32)
+    for t in tiles(d):
+        x[t] = taken[slot, t]
+        count = spread(d, total(mask[t].astype(F32)))
+        level[t] = (8.0 - count * (8.0 / d.ch)).astype(BF)
+    masked_norm(d, value_of, level, (mean, scale, share), gain, bias, low)
+    grid_to_modes(d, at, forward, low, wide)
+    send_chunk(d, at, tables[2], wide, *grid_refs)
+
+    @pl.when((core == 0) & (at.chunk == TURN_CHUNK) & (at.step == d.steps - 1))
+    def _():
+        pl.semaphore_signal(turn, inc=1, device_id={"pipe": 1}, device_id_type=MESH)
+
+    @pl.when(at.last)
+    def _():
+        dft_fill(forward_t, False, False)
+        dft_fill(inverse, True, False)
+        dft_fill(inverse_t, True, True)
+
+        @pl.when(core == 0)
+        def _():
+            fill()
+            for piece in range(d.chunks):
+                edge_copy(piece).wait_recv()
+
+        for piece in range(d.chunks):
+            edge_copy(piece).wait_send()
+        for copy in weight_copies(core):
+            copy.wait_send()
+        for copy in weight_locals():
+            copy.wait()
+
+    finish_chunks(d, at, *grid_refs)
+
+
+def point_middle(
+    d, at, wide_in, wide, x, level, gains, biases, w_in, b_in, w_out, b_out, inverse, forward,
+    residual, output, low, acc, hid, act, mean, scale, share
+):
+    gain, bias = gains[0, 1:2], biases[0, 1:2]
+    modes_to_grid(d, at, inverse, wide_in, acc)
+    for t in tiles(d):
+        value = x[t].astype(F32) + acc[t]
+        residual[t] = value
+        mean[t] = spread(d, total(value)) * (1.0 / d.ch)
+    value_of = lambda t: residual[t]
+    plain_spreads(d, value_of, mean, scale)
+    plain_values(d, value_of, mean, scale, gain, bias, low)
+    hid[...] = matmul(low[...], w_in[0])
+    for t in tiles(d):
+        act[t] = gelu_value(hid[t] + b_in[0]).astype(BF)
+    acc[...] = matmul(act[...], w_out[0])
+    for t in tiles(d):
+        output[t] = residual[t] + (acc[t] + b_out[0])
+    masked_norm(
+        d, lambda t: output[t], level, (mean, scale, share), gains[1, 0:1], biases[1, 0:1], low
+    )
+    grid_to_modes(d, at, forward, low, wide)
+
+
+def feed_back(d, layer, sums, refs, low, glow, hid, dact, act, dlow, grads):
+    w_in, b_in, w_out = refs
+    g_w_in, g_b_in, g_w_out = grads
+    hid[...] = matmul(low[...], w_in[layer])
+    dact[...] = matmul_nt(glow[...], w_out[layer])
+    for t in tiles(d):
+        active, slope = gelu_both(hid[t] + b_in[layer])
+        act[t] = active.astype(BF)
+        d_hidden = dact[t] * slope
+        sums.add(g_b_in, d_hidden)
+        dlow[t] = d_hidden.astype(BF)
+    g_w_out[...] += matmul_tn(act[...], glow[...])
+    g_w_in[...] += matmul_tn(low[...], dlow[...])
+
+
+def point_turn(
+    d, at, wide_in, wide, x, held, arrived, gains, biases, w_in, b_in, w_out, b_out, inverse, inverse_t,
+    output, d_residual, g_w_in, g_b_in, g_w_out, g_b_out, g_gain, g_bias,
+    low, glow, acc, back_acc, hid, dact, act, dlow, mean, scale, first, second
+):
+    lower = lax.axis_index("pipe") == 0
+    gain, bias = gains[1, 1:2], biases[1, 1:2]
+    stats = (mean, scale, first, second)
+    sums = Sums()
+    modes_to_grid(d, at, inverse, wide_in, acc)
+    for t in tiles(d):
+        value = x[t] + acc[t]
+        acc[t] = value
+        mean[t] = spread(d, total(value)) * (1.0 / d.ch)
+        glow[t] = jnp.where(lower, arrived[t], held[0, t])
+    value_of = lambda t: acc[t]
+    plain_spreads(d, value_of, mean, scale)
+    plain_values(d, value_of, mean, scale, gain, bias, low)
+    feed_back(
+        d, 1, sums, (w_in, b_in, w_out), low, glow, hid, dact, act, dlow,
+        (g_w_in, g_b_in, g_w_out),
+    )
+    back_acc[...] = matmul_nt(dlow[...], w_in[1])
+    dact[:, : d.ch] = matmul(act[...], w_out[1])
+    plain_back_sums(d, value_of, back_acc, gain, stats)
+    for t in tiles(d):
+        value = acc[t]
+        final = value + (dact[t, : d.ch] + b_out[1])
+        output[0, t] = final.astype(BF)
+        upper = glow[t].astype(F32)
+        sums.add(g_b_out, upper)
+        grad = back_acc[t]
+        back, unit_grad = plain_back_value(d, t, value, grad, gain, stats)
+        sums.add(g_gain, unit_grad)
+        sums.add(g_bias, grad)
+        back = upper + back
+        d_residual[t] = back
+        low[t] = back.astype(BF)
+    sums.store()
+    grid_to_modes(d, at, inverse_t, low, wide)
+
+
+def point_back(
+    d, at, wide_in, wide, x, level, d_above, residual, gains, biases, w_in, b_in, w_out, forward_t, inverse_t,
+    d_residual, g_w_in, g_b_in, g_w_out, g_b_out, g_gain, g_bias, g_gain_above, g_bias_above,
+    low, glow, acc, hid, dact, act, dlow, mean, scale, first, second
+):
+    gain, bias = gains[0, 1:2], biases[0, 1:2]
+    gain_above = gains[1, 0:1]
+    stats = (mean, scale, first, second)
+    sums = Sums()
+    modes_to_grid(d, at, forward_t, wide_in, acc)
+    masked_back_sums(d, lambda t: x[t], acc, level, gain_above, stats)
+    for t in tiles(d):
+        back, unit_grad, live_grad = masked_back_value(d, t, x[t], acc[t], level, gain_above, stats)
+        sums.add(g_gain_above, unit_grad)
+        sums.add(g_bias_above, live_grad)
+        upper = d_above[t] + back
+        sums.add(g_b_out, upper)
+        d_residual[t] = upper
+        glow[t] = upper.astype(BF)
+    value_of = lambda t: residual[t]
+    plain_sums(d, value_of, mean)
+    plain_spreads(d, value_of, mean, scale)
+    plain_values(d, value_of, mean, scale, gain, bias, low)
+    feed_back(
+        d, 0, sums, (w_in, b_in, w_out), low, glow, hid, dact, act, dlow,
+        (g_w_in, g_b_in, g_w_out),
+    )
+    acc[...] = matmul_nt(dlow[...], w_in[0])
+    plain_back_sums(d, value_of, acc, gain, stats)
+    for t in tiles(d):
+        grad = acc[t]
+        back, unit_grad = plain_back_value(d, t, residual[t], grad, gain, stats)
+        sums.add(g_gain, unit_grad)
+        sums.add(g_bias, grad)
+        back = d_residual[t] + back
+        d_residual[t] = back
+        low[t] = back.astype(BF)
+    sums.store()
+    grid_to_modes(d, at, inverse_t, low, wide)
+
+
+GRADS = 16
+GATHER_STEP = 2
+SPREAD_STEP = 12
+
+
+def build_parts(d, grads, parts):
+    for layer, held in enumerate((grads[:7], grads[7:])):
+        w_in, b_in, w_out, b_out, gain, bias, filters, *above = held
+        row = lambda ref, at=0: jnp.sum(ref[:, at : at + d.ch], axis=0, keepdims=True)
+        blank = jnp.zeros((2, d.ch), F32)
+        first = [row(above[0]), row(above[1])] if above else [blank[:1], blank[1:]]
+        small = [first[0], row(gain), first[1], row(bias), row(b_out)]
+        small += [row(b_in, at) for at in range(0, d.ff, d.ch)]
+        small = jnp.concatenate(small + [jnp.zeros((16 - len(small), d.ch), F32)], axis=0).astype(BF)
+        for band in range(d.bands):
+            index = layer * d.bands + band
+            at = 0
+            rows = d.ch // d.bands
+            for lane in range(0, d.ff, d.ch):
+                value = w_in[band * rows : (band + 1) * rows, lane : lane + d.ch]
+                parts[index, at : at + rows] = value.astype(BF)
+                at += rows
+            rows = d.ff // d.bands
+            parts[index, at : at + rows] = w_out[band * rows : (band + 1) * rows].astype(BF)
+            at += rows
+            lane = band * d.ch // d.bands // 128 * 128
+            for part in range(2):
+                value = filters[part, :, lane : lane + 128]
+                parts[index, at : at + d.degrees, part * 128 : part * 128 + 128] = value.astype(BF)
+            at += d.degrees
+            parts[index, at : at + 16] = small
+
+
+def part_rows(d):
+    return d.ff // d.bands * 2 + d.degrees + 16
+
+
+GRADS = 15
+GATHER_STEP = 4
+SPREAD_STEP = 10
+
+
+def end_kernel(d, plane, groups, *refs):
+    spectral_refs, refs = refs[:7], refs[7:]
+    x, level, d_above, gains, forward_t, start_table = refs[:6]
+    grads, refs = refs[6 : 6 + GRADS], refs[6 + GRADS :]
+    (
+        held_in, ends, result, rest, returned,
+        acc, mean, scale, first, second, g_filter, wide_in, send, order_high, arrived, arrived_high,
+        reply, reply_out, reply_in,
+        parts, pair_landed, pair_sum, landed, sum_low, spread_low,
+        rest_own, rest_landed, rest_sum, rest_spread,
+        out_p, in_p, out_a, in_a, out_b, in_b, out_c, in_c, out_d, in_d, *sems,
+    ) = refs
+    core, space, dp = lax.axis_index("pipe"), lax.axis_index("space"), lax.axis_index("dp")
+    me = core * d.bands + space
+    number = pl.program_id(0)
+    grads = grads[:6] + (g_filter,) + grads[6:]
+
+    def plane_device(index):
+        return {"pipe": index // d.bands, "space": lax.rem(index, d.bands)}
+
+    def copies_to(count, own, device, source, target, outs, ins):
+        copies = []
+        for shift in range(1, count):
+            peer = lax.rem(own + shift, count)
+            copies.append(
+                pltpu.make_async_remote_copy(
+                    src_ref=source(peer),
+                    dst_ref=target.at[shift - 1],
+                    send_sem=outs.at[shift - 1],
+                    recv_sem=ins.at[shift - 1],
+                    device_id=device(peer),
+                    device_id_type=MESH,
+                )
+            )
+        return copies
+
+    def pair_parts():
+        part = pl.ds((1 - core) * d.bands, d.bands)
+        return pair_copy(parts.at[part], pair_landed, out_p.at[0], in_p.at[0])
+
+    def band_parts():
+        return copies_to(
+            d.bands, space, lambda peer: {"space": peer}, lambda peer: pair_sum.at[peer],
+            landed, out_a, in_a,
+        )
+
+    def shares():
+        return copies_to(
+            groups, dp, lambda peer: {"dp": peer}, lambda peer: sum_low, spread_low, out_b, in_b
+        )
+
+    def rest_copies():
+        return copies_to(
+            plane, me, plane_device, lambda peer: rest_own, rest_landed, out_c, in_c
+        )
+
+    def rest_shares():
+        return copies_to(
+            groups, dp, lambda peer: {"dp": peer}, lambda peer: rest_sum, rest_spread, out_d, in_d
+        )
+
+    def reply_copy(piece, source):
+        part = pl.ds(piece * d.rows * d.lon, d.rows * d.lon)
+        return pair_copy(source.at[part], returned.at[part], reply_out.at[piece], reply_in.at[piece])
+
+    order_refs = (send, order_high, arrived, arrived_high, sems[:3], sems[3:])
+    steps = order_steps(d)
+
+    @pl.when(number == 0)
+    def _():
+        clear(rest_own, g_filter)
+        barrier = pltpu.get_barrier_semaphore()
+        for shift in range(1, plane):
+            pl.semaphore_signal(
+                barrier, inc=1, device_id=plane_device(lax.rem(me + shift, plane)),
+                device_id_type=MESH,
+            )
+        for shift in range(1, groups):
+            pl.semaphore_signal(
+                barrier, inc=1, device_id={"dp": lax.rem(dp + shift, groups)},
+                device_id_type=MESH,
+            )
+    @pl.when(number < steps)
+    def _():
+        spectral_back(d, number, send, order_high, *spectral_refs, g_filter)
+        send_orders(d, number, plane + groups - 2, *order_refs)
+
+    @pl.when(number >= steps)
+    def _():
+        at = at_of(d, number - steps)
+
+        @pl.when(at.number == 0)
+        def _():
+            build_parts(d, grads, parts)
+            pair_parts().start()
+
+            @pl.when(core == 0)
+            def _():
+                for piece in range(d.chunks):
+                    reply_copy(piece, held_in.at[1]).start()
+
+        take_chunk(d, at, start_table, *order_refs, wide_in)
+        gain = gains[0, 0:1]
+        modes_to_grid(d, at, forward_t, wide_in, acc)
+        gain_sum, bias_sum = 0.0, 0.0
+        points = d.sub * d.lon
+        stats = (mean, scale, first, second)
+        value_of = lambda t: x[t].astype(F32)
+        masked_back_sums(d, value_of, acc, level, gain, stats)
+        for t in tiles(d):
+            back, unit_grad, live_grad = masked_back_value(
+                d, t, value_of(t), acc[t], level, gain, stats
+            )
+            gain_sum = gain_sum + folded(unit_grad)
+            bias_sum = bias_sum + folded(live_grad)
+            begin = d_above[t] + back
+            begin = begin.astype(BF)
+            ends[0, t] = begin
+            row = pl.multiple_of(at.number * points + t.start, TILE)
+            reply[pl.ds(row, TILE)] = begin
+        rest_own[0:8] += gain_sum
+        rest_own[8:16] += bias_sum
+
+        @pl.when((core == 1) & (at.step == d.steps - 1))
+        def _():
+            reply_copy(at.chunk, reply).start()
+
+        @pl.when(at.number == GATHER_STEP)
+        def _():
+            pair_parts().wait_recv()
+            for band in range(d.bands):
+                value = parts[core * d.bands + band].astype(F32) + pair_landed[band].astype(F32)
+                pair_sum[band] = value.astype(BF)
+            for copy in band_parts():
+                copy.start()
+
+        @pl.when(at.number == SPREAD_STEP)
+        def _():
+            for copy in band_parts():
+                copy.wait_recv()
+            value = pair_sum[space].astype(F32)
+            for shift in range(1, d.bands):
+                value = value + landed[shift - 1].astype(F32)
+            sum_low[...] = value.astype(BF)
+            for copy in shares():
+                copy.start()
+
+        @pl.when(at.last)
+        def _():
+            for copy in rest_copies():
+                copy.start()
+            for copy in shares():
+                copy.wait_recv()
+            value = sum_low[...].astype(F32)
+            for shift in range(1, groups):
+                value = value + spread_low[shift - 1].astype(F32)
+            result[...] = value
+            for copy in rest_copies():
+                copy.wait_recv()
+            value = rest_own[...]
+            for shift in range(1, plane):
+                value = value + rest_landed[shift - 1]
+            rest_sum[...] = value
+            for copy in rest_shares():
+                copy.start()
+            for copy in rest_shares():
+                copy.wait_recv()
+            value = rest_sum[...]
+            for shift in range(1, groups):
+                value = value + rest_spread[shift - 1]
+            rest[...] = value
+            pair_parts().wait_send()
+            for copy in band_parts() + rest_copies() + shares() + rest_shares():
+                copy.wait_send()
+            for piece in range(d.chunks):
+
+                @pl.when(core == 0)
+                def _():
+                    reply_copy(piece, held_in.at[1]).wait_send()
+
+                @pl.when(core == 1)
+                def _():
+                    reply_copy(piece, reply).wait_send()
+
+                reply_copy(piece, held_in.at[1]).wait_recv()
+
+
+def fused_kernel(d, spectral_part, point_part, counts, cleared, *refs):
+    groups, at = [], 0
+    for count in counts:
+        groups.append(refs[at : at + count])
+        at += count
+    spectral_in, (start_table, end_table), point_in, spectral_out, point_out, scratch = groups
+    (
+        landed, landed_high, wide_in, wide, send, send_high, relay, order_high, arrived,
+        arrived_high, *sems,
+    ) = refs[at:]
+    order_refs = (send, order_high, arrived, arrived_high, sems[:3], sems[3:6])
+    grid_refs = (send, send_high, relay, landed, landed_high, sems[6:9], sems[9:])
+    number = pl.program_id(0)
+    steps = order_steps(d)
+
+    @pl.when(number == 0)
+    def _():
+        greet(d.bands)
+        clear(*[(spectral_out + point_out)[n] for n in cleared])
+
+    @pl.when(number < steps)
+    def _():
+        spectral_part(d, number, send, order_high, *spectral_in, *spectral_out)
+        send_orders(d, number, d.bands - 1, *order_refs)
+
+    @pl.when(number >= steps)
+    def _():
+        at = at_of(d, number - steps)
+        take_chunk(d, at, start_table, *order_refs, wide_in)
+        point_part(d, at, wide_in, wide, *point_in, *point_out, *scratch)
+        send_chunk(d, at, end_table, wide, *grid_refs)
+        finish_chunks(d, at, *grid_refs)
+
+
+def point_index(d, i, lead):
+    return jnp.maximum(i - order_steps(d), 0) if lead else i
+
+
+def sub_spec(d, minor, lead=True):
+    return pl.BlockSpec((d.sub * d.lon, minor), lambda i: (point_index(d, i, lead), 0))
+
+
+def half_spec(d, index):
+    return pl.BlockSpec((1, d.sub * d.lon, d.ch), lambda i: (index, point_index(d, i, True), 0))
+
+
+def whole_spec(shape):
+    return pl.BlockSpec(shape, lambda *_: (0,) * len(shape))
+
+
+ANY_SPEC = pl.BlockSpec(memory_space=pl.ANY)
+
+
+def sum_shape(d, width):
+    return jax.ShapeDtypeStruct((8, width), F32)
+
+
+def wide_scratch(d):
+    return pltpu.VMEM((d.ch // 128, d.rows * lat_stride(d), 128), F32)
+
+
+def step_scratch(d, minor, kind):
+    return pltpu.VMEM((d.sub * d.lon, minor), kind)
+
+
+def chunk_scratch(d):
+    return pltpu.VMEM((d.chunks, d.bands, d.own, 2 * d.rows, d.ch), BF)
+
+
+def point_cost(d, matmuls, arrays):
+    points = d.lat * d.lon
+    return pl.CostEstimate(
+        flops=int(2 * points * matmuls), bytes_accessed=int(points * d.ch * arrays),
+        transcendentals=points * d.ff,
+    )
+
+
+def landed_shapes(d):
+    return [
+        jax.ShapeDtypeStruct((d.bands, d.low, 2 * d.lat, d.ch), BF),
+        jax.ShapeDtypeStruct((d.bands, high_total(d), d.ch), BF),
+    ]
+
+
+def relay_scratch(d):
+    return pltpu.VMEM((2, max(part.size for part in high_halves(d)), d.ch), BF)
+
+
+def high_scratch(d, blocks=None):
+    shape = (high_total(d), d.ch)
+    return pltpu.VMEM(shape if blocks is None else (blocks,) + shape, BF)
+
+
+def group_index(d, i):
+    return jnp.clip(i - 1, 0, d.low // d.group - 1)
+
+
+def order_specs(d, layer, sent, tables, coefficients=()):
+    analysis, synthesis, filters = tables
+    table_spec = pl.BlockSpec(
+        (d.group, d.degrees, d.bands * d.lat), lambda i: (group_index(d, i), 0, 0)
+    )
+    block_spec = pl.BlockSpec(
+        (d.bands, d.group, 2 * d.lat, d.ch), lambda i: (0, group_index(d, i), 0, 0)
+    )
+    specs = [(sent[0], block_spec), (sent[1], None)]
+    filter_spec = pl.BlockSpec((1,) + filters.shape[1:], lambda i: (layer, 0, 0, 0))
+    specs += [(analysis, table_spec), (synthesis, table_spec), (filters, filter_spec)]
+    if coefficients:
+        specs += [(coefficients[0], coefficient_spec(d)), (coefficients[1], None)]
+    return specs
+
+
+def coefficient_spec(d):
+    return pl.BlockSpec(
+        (d.group, d.degrees, 2 * d.ch), lambda i: (group_index(d, i), 0, 0)
+    )
+
+
+def specs_of(pairs):
+    return [spec if spec is not None else whole_spec(value.shape) for value, spec in pairs]
+
+
+def fused_call(
+    d, parts, name, collective_id, spectral_in, high_tables, point_in, spectral_out,
+    point_out, scratch, cleared, cost,
+):
+    high_tables = [(table, None) for table in high_tables]
+    inputs, outputs = spectral_in + high_tables + point_in, spectral_out + point_out
+    counts = [len(v) for v in (spectral_in, high_tables, point_in, spectral_out, point_out)]
+    kernel = partial(fused_kernel, d, *parts)
+
+    def body(*refs):
+        before = sum(counts)
+        landed, after = refs[before : before + 2], refs[before + 2 :]
+        held, rest = after[: len(scratch)], after[len(scratch) :]
+        kernel(counts + [len(scratch)], cleared, *refs[:before], *held, *landed, *rest)
+
+    return pl.pallas_call(
+        body,
+        grid=(order_steps(d) + d.chunks * d.steps,),
+        in_specs=specs_of(inputs),
+        out_specs=specs_of(outputs) + [ANY_SPEC] * 2,
+        out_shape=[s for s, _ in outputs] + landed_shapes(d),
+        scratch_shapes=scratch
+        + [wide_scratch(d), wide_scratch(d), chunk_scratch(d)]
+        + [high_scratch(d, d.bands), relay_scratch(d)]
+        + [high_scratch(d), chunk_scratch(d), high_scratch(d, d.bands)]
+        + exchange_sems(d.bands, order_steps(d) + d.chunks - 2)
+        + side_sems()
+        + exchange_sems(d.bands, d.chunks)
+        + side_sems(),
+        compiler_params=pltpu.CompilerParams(
+            vmem_limit_bytes=VMEM_BYTES,
+            collective_id=collective_id,
+            has_side_effects=True,
+            dimension_semantics=("arbitrary",),
+            fuse_transposed_lhs_in_matmul=True,
+        ),
+        cost_estimate=cost,
+        name=name,
+    )(*[a for a, _ in inputs])
+
+
+def order_rows(d, block, m):
+    value = block[:, m].astype(F32).reshape(2 * d.bands * d.lat, d.ch)
+    return jnp.concatenate([part.astype(BF) for part in split_parts(d, value)], axis=1)
+
+
+def place_order(d, m, value, send):
+    rows = join_parts(d, value[:, : d.ch], value[:, d.ch :]).astype(BF)
+    for band in range(d.bands):
+        for chunk in range(d.chunks):
+            at = (band * d.chunks + chunk) * 16
+            send[chunk, band, m] = rows[at : at + 16]
+
+
+def filtered(re, im, real, imag):
+    return re * real - im * imag, re * imag + im * real
+
+
+def filtered_back(dr, di, real, imag):
+    return dr * real + di * imag, di * real - dr * imag
+
+
+def spectral(
+    d, step, send, send_high, block, block_high, analysis, synthesis, filters,
+    coefficients, coefficients_high,
+):
+    bands = (lax.axis_index("space"),) + sides()[:2]
+
+    @pl.when(step == 0)
+    def _():
+        for _, count, at in high_rows(d):
+            rows = slice(at, at + 2 * count)
+            value = sum(block_high[band, rows].astype(F32) for band in bands)
+            coefficients_high[rows] = value
+            real, imag = (filters[0, part, d.degrees - count :] for part in range(2))
+            value = filtered(*split_parts(d, value), real, imag)
+            send_high[rows] = join_parts(d, *value).astype(BF)
+
+    @pl.when(step > 0)
+    def _():
+        real, imag = filters[0, 0], filters[0, 1]
+        for m in range(d.group):
+            value = matmul(analysis[m], order_rows(d, block, m))
+            coefficients[m] = value
+            value = filtered(value[:, : d.ch], value[:, d.ch :], real, imag)
+            value = jnp.concatenate([part.astype(BF) for part in value], axis=1)
+            place_order(d, (step - 1) * d.group + m, matmul_tn(synthesis[m], value), send)
+
+
+def spectral_back(
+    d, step, send, send_high, block, block_high, analysis, synthesis, filters,
+    coefficients, coefficients_high, g_filter,
+):
+    bands = (lax.axis_index("space"),) + sides()[:2]
+
+    @pl.when(step == 0)
+    def _():
+        for _, count, at in high_rows(d):
+            rows = slice(at, at + 2 * count)
+            lo = d.degrees - count
+            value = sum(block_high[band, rows].astype(F32) for band in bands)
+            dr, di = split_parts(d, value)
+            re, im = split_parts(d, coefficients_high[rows])
+            g_filter[0, lo:] += re * dr + im * di
+            g_filter[1, lo:] += re * di - im * dr
+            real, imag = (filters[0, part, lo:] for part in range(2))
+            send_high[rows] = join_parts(d, *filtered_back(dr, di, real, imag)).astype(BF)
+
+    @pl.when(step > 0)
+    def _():
+        real, imag = filters[0, 0], filters[0, 1]
+        for m in range(d.group):
+            value = matmul(synthesis[m], order_rows(d, block, m))
+            dr, di = value[:, : d.ch], value[:, d.ch :]
+            re, im = coefficients[m, :, : d.ch], coefficients[m, :, d.ch :]
+            g_filter[0] += re * dr + im * di
+            g_filter[1] += re * di - im * dr
+            value = filtered_back(dr, di, real, imag)
+            value = jnp.concatenate([part.astype(BF) for part in value], axis=1)
+            place_order(d, (step - 1) * d.group + m, matmul_tn(analysis[m], value), send)
+
+
+def point_start_call(d, edges, mask, own_weights, orders):
+    points = d.lat * d.lon
+    flat = jax.ShapeDtypeStruct((points, d.ch), BF)
+    table = jax.ShapeDtypeStruct((d.low, d.degrees, d.degrees), BF)
+    high = jax.ShapeDtypeStruct((d.bands * d.high, d.lat, d.lat), BF)
+    fulls = [jax.ShapeDtypeStruct((2,) + w.shape[1:], w.dtype) for w in own_weights]
+    gains, biases = own_weights[:2]
+    dft = jax.ShapeDtypeStruct((2 * d.own * d.bands, d.lon), BF)
+    dma = pltpu.SemaphoreType.DMA
+    own = orders.shape[0] - d.bands * d.high
+    width = -(-d.degrees // 128) * 128
+    rows = max(d.degrees * own, d.lat * d.bands * d.high)
+    return pl.pallas_call(
+        partial(point_start_kernel, d),
+        grid=(d.chunks * d.steps,),
+        in_specs=[
+            ANY_SPEC,
+            sub_spec(d, d.ch, False),
+            whole_spec(gains.shape),
+            whole_spec(biases.shape),
+            whole_spec(orders.shape),
+        ]
+        + [ANY_SPEC] * WEIGHTS,
+        out_specs=[sub_spec(d, d.ch, False), sub_spec(d, 128, False)]
+        + [whole_spec(table.shape)] * 2
+        + [whole_spec(high.shape)] * 2
+        + [whole_spec(dft.shape)] * 4
+        + [ANY_SPEC] * (WEIGHTS + 3),
+        out_shape=[flat, jax.ShapeDtypeStruct((points, 128), BF), table, table, high, high]
+        + [dft] * 4
+        + [flat]
+        + fulls
+        + landed_shapes(d),
+        scratch_shapes=[
+            pltpu.VMEM((2, d.sub * d.lon, d.ch), BF),
+            dma((2,)),
+            pltpu.VMEM(gains.shape, F32),
+            pltpu.VMEM(biases.shape, F32),
+            dma((WEIGHTS + 2,)),
+            dma((WEIGHTS + 2,)),
+            dma((WEIGHTS,)),
+            dma((d.chunks,)),
+            dma((d.chunks,)),
+            pltpu.SemaphoreType.REGULAR,
+            step_scratch(d, 128, F32),
+            step_scratch(d, 128, F32),
+            step_scratch(d, 128, F32),
+            pltpu.VMEM((width // 128, rows, 128), F32),
+            step_scratch(d, d.ch, BF),
+            wide_scratch(d),
+            chunk_scratch(d),
+            high_scratch(d, d.bands),
+            relay_scratch(d),
+        ]
+        + exchange_sems(d.bands, d.chunks)
+        + side_sems(),
+        compiler_params=pltpu.CompilerParams(
+            vmem_limit_bytes=VMEM_BYTES,
+            collective_id=2,
+            has_side_effects=True,
+            dimension_semantics=("arbitrary",),
+        ),
+        cost_estimate=point_cost(d, 2 * d.own * d.bands * d.ch, 8),
+        name="point_start",
+    )(edges, mask, gains, biases, orders, *own_weights)
+
+
+def end_call(d, pairs, groups, spectral_in, grid_in, whole_in, grads, held):
+    plane = pairs * d.bands
+    points = d.lat * d.lon
+    shape = (part_rows(d), d.ch)
+    rest = (16, d.ch)
+    dma = lambda count: [pltpu.SemaphoreType.DMA((max(count, 1),))] * 2
+    others = max(groups - 1, 1)
+    wholes = [(a, None) for a in whole_in + grads]
+    inputs = spectral_in + grid_in + wholes + [(held, ANY_SPEC)]
+    return pl.pallas_call(
+        partial(end_kernel, d, plane, groups),
+        grid=(order_steps(d) + d.chunks * d.steps,),
+        in_specs=specs_of(inputs),
+        out_specs=[half_spec(d, 0), whole_spec(shape), whole_spec(rest), ANY_SPEC],
+        out_shape=[
+            jax.ShapeDtypeStruct(held.shape, BF),
+            jax.ShapeDtypeStruct(shape, F32),
+            jax.ShapeDtypeStruct(rest, F32),
+            jax.ShapeDtypeStruct((points, d.ch), BF),
+        ],
+        scratch_shapes=[step_scratch(d, d.ch, F32)]
+        + [step_scratch(d, 128, F32)] * 4
+        + [
+            pltpu.VMEM((2, d.degrees, d.ch), F32),
+            wide_scratch(d),
+            chunk_scratch(d),
+            high_scratch(d),
+            chunk_scratch(d),
+            high_scratch(d, d.bands),
+            pltpu.VMEM((points, d.ch), BF),
+        ]
+        + dma(d.chunks)
+        + [
+            pltpu.VMEM((plane,) + shape, BF),
+            pltpu.VMEM((d.bands,) + shape, BF),
+            pltpu.VMEM((d.bands,) + shape, BF),
+            pltpu.VMEM((d.bands - 1,) + shape, BF),
+            pltpu.VMEM(shape, BF),
+            pltpu.VMEM((others,) + shape, BF),
+            pltpu.VMEM(rest, F32),
+            pltpu.VMEM((plane - 1,) + rest, F32),
+            pltpu.VMEM(rest, F32),
+            pltpu.VMEM((others,) + rest, F32),
+        ]
+        + dma(1)
+        + dma(d.bands - 1)
+        + dma(groups - 1)
+        + dma(plane - 1)
+        + dma(groups - 1)
+        + exchange_sems(d.bands, order_steps(d) + d.chunks - 2)
+        + side_sems(),
+        input_output_aliases={len(inputs) - 1: 0},
+        compiler_params=pltpu.CompilerParams(
+            vmem_limit_bytes=VMEM_BYTES,
+            collective_id=1,
+            has_side_effects=True,
+            dimension_semantics=("arbitrary",),
+            fuse_transposed_lhs_in_matmul=True,
+        ),
+        cost_estimate=point_cost(d, 2 * d.own * d.bands * d.ch, 18),
+        name="spectral_end",
+    )(*[a for a, _ in inputs])
+
+
+def chosen(index, pieces):
+    value = pieces[0]
+    for n in range(1, len(pieces)):
+        value = jnp.where(index == n, pieces[n], value)
+    return value
+
+
+def place_kernel(
+    d, where, held, returned, result, rest, ends, g_gain, g_bias, g_filter, g_w_in, g_b_in,
+    g_w_out, g_b_out
+):
+    core, space = where[0], where[1]
+    ends[0, core] = held[0].astype(F32)
+    ends[0, 1 - core] = returned[...].astype(F32)
+
+    @pl.when(pl.program_id(0) == 0)
+    def _():
+        at, rows = 0, d.ch // d.bands
+        for lane in range(0, d.ff, d.ch):
+            g_w_in[0, :, lane : lane + d.ch] = result[at : at + rows]
+            at += rows
+        rows = d.ff // d.bands
+        g_w_out[0] = result[at : at + rows]
+        at += rows
+        width = d.ch // d.bands
+        for part in range(2):
+            value = result[at : at + d.degrees, part * 128 : part * 128 + 128].T
+            pieces = [value[lane : lane + width] for lane in range(0, 128, width)]
+            g_filter[0, part] = chosen(lax.rem(space, len(pieces)), pieces)
+        at += d.degrees
+        small = result[at : at + 8]
+        extra = [jnp.sum(rest[part * 8 : part * 8 + 8], axis=0, keepdims=True) for part in range(2)]
+        extra = [jnp.where(core == 0, value, 0.0) for value in extra]
+        bands = range(d.bands)
+
+        def cut(row):
+            return chosen(space, [row[:, n * width : (n + 1) * width] for n in bands])
+
+        for out, first, more in ((g_gain, 0, extra[0]), (g_bias, 2, extra[1])):
+            out[0, 0:1] = cut(small[first : first + 1] + more)
+            out[0, 1:2] = cut(small[first + 1 : first + 2])
+        g_b_out[...] = cut(small[4:5])
+        hidden = [small[5 + n : 6 + n] for n in range(d.ff // d.ch)]
+        hidden = jnp.concatenate(hidden, axis=1)
+        g_b_in[...] = chosen(space, [hidden[:, n * rows : (n + 1) * rows] for n in bands])
+
+
+def place_call(d, core, space, held, returned, result, rest, rows):
+    points, ch = returned.shape
+    width = ch // d.bands
+    shapes = [
+        (1, 2, points, ch),
+        (1, 2, width),
+        (1, 2, width),
+        (1, 2, width, d.degrees),
+        (1, width, d.ff),
+        (1, d.ff // d.bands),
+        (1, d.ff // d.bands, ch),
+        (1, width),
+    ]
+    return pl.pallas_call(
+        partial(place_kernel, d),
+        grid_spec=pltpu.PrefetchScalarGridSpec(
+            num_scalar_prefetch=1,
+            grid=(points // rows,),
+            in_specs=[
+                pl.BlockSpec((1, rows, ch), lambda i, where: (where[0], i, 0)),
+                pl.BlockSpec((rows, ch), lambda i, where: (i, 0)),
+                whole_spec(result.shape),
+                whole_spec(rest.shape),
+            ],
+            out_specs=[pl.BlockSpec((1, 2, rows, ch), lambda i, where: (0, 0, i, 0))]
+            + [whole_spec(shape) for shape in shapes[1:]],
+        ),
+        out_shape=[jax.ShapeDtypeStruct(shape, F32) for shape in shapes],
+        compiler_params=pltpu.CompilerParams(vmem_limit_bytes=VMEM_BYTES),
+        name="place",
+    )(jnp.stack([core, space]).astype(jnp.int32), held, returned, result, rest)
 
 
 def swapped(value, axis, bit):
@@ -19,7 +1634,7 @@
     return jax.tree.map(lambda a: a.astype(jnp.bfloat16) if a.dtype == jnp.float32 else a, shard)
 
 
-def legendre_table(orders, degree_count, colat_count):
+def plain_legendre_table(orders, degree_count, colat_count):
     colatitude = (jnp.arange(colat_count, dtype=jnp.float32) + 0.5) * (math.pi / colat_count)
     cosine = jnp.cos(colatitude)
     sine_col = jnp.sin(colatitude)
@@ -63,7 +1678,7 @@
     return (jnp.transpose(table_rows, (1, 0, 2)), sine_col)
 
 
-def fourier_tables(order_count, lon_count):
+def plain_fourier_tables(order_count, lon_count):
     orders = jnp.arange(order_count, dtype=jnp.int32)
     points = jnp.arange(lon_count, dtype=jnp.int32)
     phase_index = orders[:, None] * points[None, :] % lon_count
@@ -134,7 +1749,7 @@
     return lax.all_to_all(joined, "space", split_axis=0, concat_axis=1, tiled=True)
 
 
-def local(edges, mask_levels, norm_gains, norm_biases, filters, w_in, bias_in, w_out, bias_out):
+def plain_local(edges, mask_levels, norm_gains, norm_biases, filters, w_in, bias_in, w_out, bias_out):
     section_index = lax.axis_index("pipe")
     band_count = lax.axis_size("space")
     micro_count = edges.shape[1]
@@ -143,12 +1758,12 @@
     lat_count = edges.shape[2] * band_count
     order_count = lon_count // 2
     live_mask = mask_levels.astype(jnp.float32)
-    forward_table, inverse_table = fourier_tables(order_count, lon_count)
+    forward_table, inverse_table = plain_fourier_tables(order_count, lon_count)
     forward_dft = forward_table.astype(jnp.bfloat16)
     inverse_dft = inverse_table.astype(jnp.bfloat16)
     order_dev = order_count // band_count
     orders = lax.axis_index("space") * order_dev + jnp.arange(order_dev, dtype=jnp.int32)
-    legendre, sine_col = legendre_table(orders, lat_count, lat_count)
+    legendre, sine_col = plain_legendre_table(orders, lat_count, lat_count)
     analysis = (legendre * (sine_col * (math.pi / lat_count))[None, None, :]).astype(jnp.bfloat16)
     synthesis = legendre.astype(jnp.bfloat16)
     gelu_tanh = partial(jax.nn.gelu, approximate=True)
@@ -378,6 +1993,112 @@
     return (ends,) + tuple((entry[None] for entry in summed))
 
 
+def local(edges, mask_levels, norm_gains, norm_biases, filters, w_in, bias_in, w_out, bias_out):
+    bands = lax.axis_size("space")
+    lat, lon, ch = edges.shape[2:]
+    odd = lat % ROWS or lat % bands or lon != 2 * lat * bands or bands != 4
+    if odd or edges.shape[1] != 2:
+        return plain_local(
+            edges, mask_levels, norm_gains, norm_biases, filters, w_in, bias_in, w_out, bias_out
+        )
+    ff = w_in.shape[2]
+    orders = lon // 2
+    own = orders // bands
+    degrees = lat * bands
+    sub = 2
+    group = 4
+    points = lat * lon
+    high_count = lat // bands
+    low_count = own - high_count
+    d = Dims(
+        bands, lat, lon, ch, own, degrees, ff, ROWS, lat // ROWS, sub, ROWS // sub, group,
+        low_count, high_count,
+    )
+    core = lax.axis_index("pipe")
+    space = lax.axis_index("space")
+    edges = edges.reshape(1, 2, points, ch)
+    mask = mask_levels.reshape(points, ch)
+
+    low_orders = space + bands * jnp.arange(-(-low_count // 8) * 8, dtype=jnp.int32)
+    step = jnp.arange(bands * high_count, dtype=jnp.int32)
+    high_orders = bands * (low_count + step % high_count) + step // high_count
+    own_weights = (
+        norm_gains, norm_biases, filters, w_in, bias_in[:, None, :], w_out, bias_out[:, None, :],
+    )
+    orders_in = legendre_orders(jnp.concatenate([low_orders, high_orders]))
+    x0, level, *made = point_start_call(d, edges, mask, own_weights, orders_in)
+    analysis, synthesis, high_analysis, high_synthesis = made[:4]
+    forward, forward_t, inverse, inverse_t, arrived = made[4:9]
+    gains, biases, filt, win, bin_, wout, bout, *sent = made[9:]
+
+    grid_f32 = (jax.ShapeDtypeStruct((points, ch), F32), sub_spec(d, ch))
+    small = lambda *arrays: [(a, None) for a in arrays]
+    grid = lambda *arrays: [(a, sub_spec(d, ch)) for a in arrays]
+    levels = [(level, sub_spec(d, 128))]
+    table = lambda a, b: jax.ShapeDtypeStruct((a, b), F32)
+    sums = lambda *widths: [(sum_shape(d, w), None) for w in widths]
+    low = step_scratch(d, ch, BF)
+    acc = step_scratch(d, ch, F32)
+    hid = step_scratch(d, ff, F32)
+    act = step_scratch(d, ff, BF)
+    stat = step_scratch(d, 128, F32)
+    dft = 2 * orders * ch
+    ffn = ch * ff
+    tables = (analysis, synthesis, filt)
+    weight_grads = [(table(ch, ff), None), (sum_shape(d, ff), None), (table(ff, ch), None)]
+    coefficients = [
+        (jax.ShapeDtypeStruct((low_count, degrees, 2 * ch), F32), coefficient_spec(d)),
+        (jax.ShapeDtypeStruct((high_total(d), ch), F32), None),
+    ]
+    filter_grad = (jax.ShapeDtypeStruct((2, degrees, ch), F32), None)
+
+    *coef0, res0, x1, sent, sent_high = fused_call(
+        d, (spectral, point_middle), "spectral_first_point_middle", 3,
+        order_specs(d, 0, sent, tables), (high_synthesis, high_analysis),
+        grid(x0) + levels + small(gains, biases, win, bin_, wout, bout, inverse, forward),
+        coefficients, [grid_f32, grid_f32],
+        [low, acc, hid, act, stat, stat, stat], (), point_cost(d, 2 * dft + 2 * ffn, 18),
+    )
+    held_shape = jax.ShapeDtypeStruct((2, points, ch), BF)
+    (
+        *coef1, held, d_res1, g_win1, g_bin1, g_wout1, g_bout1, g_gain21, g_bias21, sent,
+        sent_high,
+    ) = fused_call(
+        d, (spectral, point_turn), "spectral_second_point_turn", 4,
+        order_specs(d, 1, (sent, sent_high), tables), (high_synthesis, high_synthesis),
+        grid(x1) + [(edges[0], half_spec(d, 1))] + grid(arrived)
+        + small(gains, biases, win, bin_, wout, bout, inverse, inverse_t),
+        coefficients,
+        [(held_shape, half_spec(d, 1)), grid_f32] + weight_grads + sums(ch, ch, ch),
+        [low, low, acc, acc, hid, hid, act, act, stat, stat, stat, stat],
+        (4, 5, 6, 7, 8, 9), point_cost(d, 2 * dft + 6 * ffn, 20),
+    )
+    (
+        g_filt1, d_res0, g_win0, g_bin0, g_wout0, g_bout0, g_gain20, g_bias20, g_gain11, g_bias11,
+        sent, sent_high,
+    ) = fused_call(
+        d, (spectral_back, point_back), "spectral_back_point_back", 5,
+        order_specs(d, 1, (sent, sent_high), tables, coef1), (high_analysis, high_synthesis),
+        grid(x1) + levels + grid(d_res1, res0)
+        + small(gains, biases, win, bin_, wout, forward_t, inverse_t),
+        [filter_grad], [grid_f32] + weight_grads + sums(ch, ch, ch, ch, ch),
+        [low, low, acc, hid, hid, act, act, stat, stat, stat, stat],
+        (0, 2, 3, 4, 5, 6, 7, 8, 9), point_cost(d, 2 * dft + 5 * ffn, 24),
+    )
+    grads = (
+        g_win0, g_bin0, g_wout0, g_bout0, g_gain20, g_bias20,
+        g_win1, g_bin1, g_wout1, g_bout1, g_gain21, g_bias21, g_filt1, g_gain11, g_bias11,
+    )
+    pairs, groups = lax.axis_size("pipe"), lax.axis_size("dp")
+    held, result, rest, returned = end_call(
+        d, pairs, groups, order_specs(d, 0, (sent, sent_high), tables, coef0),
+        grid(x0) + levels + grid(d_res0), (gains, forward_t, high_analysis), grads, held
+    )
+    ends, *small_grads = place_call(d, core, space, held, returned, result, rest, 4 * lon)
+    small_grads[2] = jnp.swapaxes(small_grads[2], 2, 3)
+    return (ends.reshape(1, 2, lat, lon, ch), *small_grads)
+
+
 def solution(mesh):
     return jax.shard_map(
         local,

time: 2730 us -> 811 us (0.30)
  Pallas kernels: 0 us -> 806 us
  other arithmetic: 628 us -> 0.84 us
  local copies, waits for them, and re-layouts: 546 us -> 0.72 us
  blocking collectives: 491 us -> 0 us
  matrix products: 472 us -> 0 us
  waiting for transfers between devices: 406 us -> 0 us
  loops' own time: 130 us -> 0 us
    pallas_call x0 -> x6, Pallas kernels: none -> 806 us  [the longest x3 550 us: fused_call(): pl.pallas_call(body, grid=(order_steps(d) + d.chunks * d.steps,), in_spec...]
    dot_general x28 -> x0, matrix products: 472 us -> none  [the longest x2 72.4 us: backward_layer(): jnp.einsum('pc,fc->pf', grad_low, weight_out, preferred_element_type=jnp....]
    all_to_all x4 -> x0, blocking collectives: 443 us -> none  [the longest x2 220 us: grad_to_modes(): lax.all_to_all(spectrum, 'space', split_axis=1, concat_axis=0, tiled=True)]
    reduce_sum x16 -> x0, other arithmetic: 263 us -> none  [the longest x2 43.4 us: norm_plain(): centered = values - average]
    all_to_all x4 -> x0, waiting for transfers between devices: 246 us -> none  [the longest x2 171 us: to_bands(): lax.all_to_all(joined, 'space', split_axis=0, concat_axis=1, tiled=True)]
    dynamic_update_slice x192 -> x0, other arithmetic: 141 us -> none  [legendre_table(): lax.scan(recurrence, (zero_rows, zero_rows), jnp.arange(degree_count, dty...]
    another operation x1 -> x0, loops' own time: 130 us -> none  [legendre_table(): lax.scan(recurrence, (zero_rows, zero_rows), jnp.arange(degree_count, dty...]
    dynamic_slice x192 -> x0, local copies, waits for them, and re-layouts: 112 us -> none  [legendre_table(): lax.scan(recurrence, (zero_rows, zero_rows), jnp.arange(degree_count, dty...]
  transfers between devices with their start and end apart: 15 -> 0, of which waited for: 10 -> 0; matrix products, arithmetic and copies ran while one was open for 16% -> 0% of each run, Pallas kernels for 0% -> 0%
where the time goes in v1:
time: 811 us; the launch traced here: 808 us
  Pallas kernels  806 us (99%)
    pallas_call x3, Pallas kernels, fused_call(): pl.pallas_call(body, grid=(order_steps(d) + d.chunks * d.steps,), in_spec...  550 us
    pallas_call x1, Pallas kernels, end_call(): pl.pallas_call(partial(end_kernel, d, plane, groups), grid=(order_steps(d...  139 us
    pallas_call x1, Pallas kernels, point_start_call(): pl.pallas_call(partial(point_start_kernel, d), grid=(d.chunks * d.steps,)...  96 us
    pallas_call x1, Pallas kernels, place_call(): pl.pallas_call(partial(place_kernel, d), grid_spec=pltpu.PrefetchScalarGr...  21.4 us

profile of v1, /device:TPU:0, one launch (start us, length us, event | category | flops | bytes accessed | tf_op | source)
XLA Modules:
  0.0 808.2 jit_solution(15867917640930819239)
XLA Ops:
  0.6 0.7 pad_add_fusion.where
  1.3 0.1 add_multiply_fusion
  1.5 0.7 copy.20.orders
  2.2 96.0 %point_start.1 = (bf16[18432,256]{1,0:T(8,128)(2,1)}, bf16[18432,128]{1,0:T(8,128)(2,1)}, bf16[36,192,192]{2,1,0:T(8,128)(2,1)}, bf16[36,192,192]{2,1,0:T(8,128)...) custom-call(bf16[1,2,18432,256]{3,2,1,0:T(8,128)(2,1)} %bitcast.14, ...), custom_call_target="tpu_custom_call" | custom-call | flops 3623878656 | bytes 37748736 | tf_op jit(solution)/shard_map/point_start/pallas_call | solution.py:1428
  98.2 182.8 %spectral_first_point_middle.1 = (f32[36,192,512]{2,1,0:T(8,128)}, f32[672,256]{1,0:T(8,128)}, f32[18432,256]{1,0:T(8,128)}, f32[18432,256]{1,0:T(8,128)}, bf16[...) custom-call(bf16[4,36,96,256]{3,2,1,0:T(8,128)(2,1)} %get-tuple-element.70.refs_0_, ...), custom_call_target="tpu_custom_call" | custom-call | flops 16911433728 | bytes 84934656 | tf_op jit(solution)/shard_map/spectral_first_point_middle/pallas_call | solution.py:1309
  281.1 184.3 %spectral_second_point_turn.1 = (f32[36,192,512]{2,1,0:T(8,128)}, f32[672,256]{1,0:T(8,128)}, bf16[2,18432,256]{2,1,0:T(8,128)(2,1)}, f32[18432,256]{1,0:T(8,128...) custom-call(bf16[4,36,96,256]{3,2,1,0:T(8,128)(2,1)} %get-tuple-elem, ...), custom_call_target="tpu_custom_call" | custom-call | flops 36238786560 | bytes 94371840 | tf_op jit(solution)/shard_map/spectral_second_point_turn/pallas_call | solution.py:1309
  465.3 182.6 %spectral_back_point_back.1 = (f32[2,192,256]{2,1,0:T(8,128)}, f32[18432,256]{1,0:T(8,128)}, f32[256,512]{1,0:T(8,128)}, f32[8,512]{1,0:T(8,128)}, f32[512,256]{...) custom-call(bf16[4,36,96,256]{3,2,1,0:T(8,128)(2,1)} %get-tuple-elem, ...), custom_call_target="tpu_custom_call" | custom-call | flops 31406948352 | bytes 113246208 | tf_op jit(solution)/shard_map/spectral_back_point_back/pallas_call | solution.py:1309
  648.0 138.6 %spectral_end.1 = (bf16[2,18432,256]{2,1,0:T(8,128)(2,1)}, f32[464,256]{1,0:T(8,128)}, f32[16,256]{1,0:T(8,128)}, bf16[18432,256]{1,0:T(8,128)(2,1)}) custom-call(bf16[4,36,96,256]{3,2,1,0:T(8,128)(2,1)} %get-tuple-element.99.refs_0_, bf16[4,672,256]{2,1,0:T(8,128)(2,1)} %get-tuple-element.100.refs_1_, ...), custom_call_target="tpu_custom_call", output_to_operand_aliasing={{0}: (28, {})} | custom-call | flops 3623878656 | bytes 84934656 | tf_op jit(solution)/shard_map/spectral_end/pallas_call | solution.py:1492
  786.6 21.4 %place.1 = (f32[1,2,18432,256]{3,2,1,0:T(8,128)}, f32[1,2,64]{2,1,0:T(2,128)}, f32[1,2,64]{2,1,0:T(2,128)}, f32[1,2,64,192]{3,2,1,0:T(8,128)}, f32[1,64,512]{2,1...) custom-call(s32[2]{0:T(128)} %pad_add_fusion.where, ...), custom_call_target="tpu_custom_call" | custom-call | tf_op jit(solution)/shard_map/place/pallas_call | solution.py:1607
  (3 shorter events, 0.0 us)

commit v2 on v1

--- a/solution.py
+++ b/solution.py
@@ -587,16 +587,20 @@
     return 1 + d.low // d.group
 
 
+def order_piece_count(d):
+    return EARLY_CHUNKS * (order_steps(d) - 1) + d.chunks - EARLY_CHUNKS
+
+
 def order_pieces(d, send, arrived, sems):
-    count = order_steps(d)
-
-    def first(step):
+    groups = order_steps(d) - 1
+
+    def first(step, chunk):
         part = pl.ds((step - 1) * d.group, d.group)
         return (
             d.bands,
-            step - 1,
-            lambda peer: send.at[0, peer, part],
-            lambda band: arrived.at[0, band, part],
+            chunk * groups + step - 1,
+            lambda peer: send.at[chunk, peer, part],
+            lambda band: arrived.at[chunk, band, part],
             sems,
         )
 
@@ -604,7 +608,7 @@
         part = pl.ds(0, d.low)
         return (
             d.bands,
-            count + chunk - 2,
+            EARLY_CHUNKS * groups + chunk - EARLY_CHUNKS,
             lambda peer: send.at[chunk, peer, part],
             lambda band: arrived.at[chunk, band, part],
             sems,
@@ -614,6 +618,7 @@
 
 
 PASS_STEP = 5
+EARLY_CHUNKS = 2
 
 
 def send_orders(d, step, peer_count, send, order_high, arrived, arrived_high, sems, high_sems):
@@ -628,7 +633,8 @@
 
     @pl.when(step > 0)
     def _():
-        start_piece(*first(step))
+        for chunk in range(EARLY_CHUNKS):
+            start_piece(*first(step, chunk))
 
     @pl.when(step == PASS_STEP)
     def _():
@@ -639,7 +645,7 @@
 
     @pl.when(step == order_steps(d) - 1)
     def _():
-        for chunk in range(1, d.chunks):
+        for chunk in range(EARLY_CHUNKS, d.chunks):
             start_piece(*whole(chunk))
 
 
@@ -654,14 +660,19 @@
                 copy.wait_recv()
             spread_own(order_high, arrived_high, high_sems).wait()
             degrees_to_rows(d, table, arrived_high, arrived)
-            for step in range(1, order_steps(d)):
-                finish_piece(*first(step))
             for copy in spread_copies(
                 d, order_high, arrived_high, high_sems, False
             ) + passing_copies(d, arrived_high, high_sems, False):
                 copy.wait_send()
 
-        @pl.when(at.chunk > 0)
+        for chunk in range(EARLY_CHUNKS):
+
+            @pl.when(at.chunk == chunk)
+            def _():
+                for step in range(1, order_steps(d)):
+                    finish_piece(*first(step, chunk))
+
+        @pl.when(at.chunk >= EARLY_CHUNKS)
         def _():
             finish_piece(*whole(at.chunk))
 
@@ -748,6 +759,11 @@
         lows = orders[: orders.shape[0] - d.bands * d.high]
         legendre_fill(0, lows, d.degrees, 0, *tables[:2], legendre_rows)
 
+    def fill_high():
+        highs = orders[orders.shape[0] - d.bands * d.high :]
+        first_lat = lax.axis_index("space") * d.lat
+        legendre_fill(d.degrees - d.lat, highs, d.degrees, first_lat, *tables[2:], legendre_rows)
+
     @pl.when(number == 0)
     def _():
         barrier = pltpu.get_barrier_semaphore()
@@ -760,13 +776,11 @@
         for piece in range(d.chunks):
             edge_copy(piece).start()
         dft_fill(forward, False, True)
-        highs = orders[orders.shape[0] - d.bands * d.high :]
-        first_lat = lax.axis_index("space") * d.lat
-        legendre_fill(d.degrees - d.lat, highs, d.degrees, first_lat, *tables[2:], legendre_rows)
 
         @pl.when(core == 1)
         def _():
             fill()
+            fill_high()
             pl.semaphore_wait(turn, 1)
 
         start_take(0)
@@ -788,6 +802,11 @@
         level[t] = (8.0 - count * (8.0 / d.ch)).astype(BF)
     masked_norm(d, value_of, level, (mean, scale, share), gain, bias, low)
     grid_to_modes(d, at, forward, low, wide)
+
+    @pl.when((core == 0) & at.last)
+    def _():
+        fill_high()
+
     send_chunk(d, at, tables[2], wide, *grid_refs)
 
     @pl.when((core == 0) & (at.chunk == TURN_CHUNK) & (at.step == d.steps - 1))
@@ -1316,7 +1335,7 @@
         + [wide_scratch(d), wide_scratch(d), chunk_scratch(d)]
         + [high_scratch(d, d.bands), relay_scratch(d)]
         + [high_scratch(d), chunk_scratch(d), high_scratch(d, d.bands)]
-        + exchange_sems(d.bands, order_steps(d) + d.chunks - 2)
+        + exchange_sems(d.bands, order_piece_count(d))
         + side_sems()
         + exchange_sems(d.bands, d.chunks)
         + side_sems(),
@@ -1529,7 +1548,7 @@
         + dma(groups - 1)
         + dma(plane - 1)
         + dma(groups - 1)
-        + exchange_sems(d.bands, order_steps(d) + d.chunks - 2)
+        + exchange_sems(d.bands, order_piece_count(d))
         + side_sems(),
         input_output_aliases={len(inputs) - 1: 0},
         compiler_params=pltpu.CompilerParams(

time: 811 us -> 810 us (level)
  no operation moved by 1% of the time
where the time goes in v2:
time: 810 us; the launch traced here: 808 us
  Pallas kernels  806 us (100%)
    pallas_call x3, Pallas kernels, fused_call(): pl.pallas_call(body, grid=(order_steps(d) + d.chunks * d.steps,), in_spec...  546 us
    pallas_call x1, Pallas kernels, end_call(): pl.pallas_call(partial(end_kernel, d, plane, groups), grid=(order_steps(d...  145 us
    pallas_call x1, Pallas kernels, point_start_call(): pl.pallas_call(partial(point_start_kernel, d), grid=(d.chunks * d.steps,)...  93.1 us
    pallas_call x1, Pallas kernels, place_call(): pl.pallas_call(partial(place_kernel, d), grid_spec=pltpu.PrefetchScalarGr...  21.4 us

profile of v2, /device:TPU:0, one launch (start us, length us, event | category | flops | bytes accessed | tf_op | source)
XLA Modules:
  0.0 808.1 jit_solution(16646915302900528940)
XLA Ops:
  0.6 0.7 pad_add_fusion.where
  1.3 0.1 add_multiply_fusion
  1.5 0.7 copy.20.orders
  2.2 93.1 %point_start.1 = (bf16[18432,256]{1,0:T(8,128)(2,1)}, bf16[18432,128]{1,0:T(8,128)(2,1)}, bf16[36,192,192]{2,1,0:T(8,128)(2,1)}, bf16[36,192,192]{2,1,0:T(8,128)...) custom-call(bf16[1,2,18432,256]{3,2,1,0:T(8,128)(2,1)} %bitcast.14, ...), custom_call_target="tpu_custom_call" | custom-call | flops 3623878656 | bytes 37748736 | tf_op jit(solution)/shard_map/point_start/pallas_call | solution.py:1447
  95.3 181.1 %spectral_first_point_middle.1 = (f32[36,192,512]{2,1,0:T(8,128)}, f32[672,256]{1,0:T(8,128)}, f32[18432,256]{1,0:T(8,128)}, f32[18432,256]{1,0:T(8,128)}, bf16[...) custom-call(bf16[4,36,96,256]{3,2,1,0:T(8,128)(2,1)} %get-tuple-element.70.refs_0_, ...), custom_call_target="tpu_custom_call" | custom-call | flops 16911433728 | bytes 84934656 | tf_op jit(solution)/shard_map/spectral_first_point_middle/pallas_call | solution.py:1328
  276.4 182.0 %spectral_second_point_turn.1 = (f32[36,192,512]{2,1,0:T(8,128)}, f32[672,256]{1,0:T(8,128)}, bf16[2,18432,256]{2,1,0:T(8,128)(2,1)}, f32[18432,256]{1,0:T(8,128...) custom-call(bf16[4,36,96,256]{3,2,1,0:T(8,128)(2,1)} %get-tuple-elem, ...), custom_call_target="tpu_custom_call" | custom-call | flops 36238786560 | bytes 94371840 | tf_op jit(solution)/shard_map/spectral_second_point_turn/pallas_call | solution.py:1328
  458.4 182.8 %spectral_back_point_back.1 = (f32[2,192,256]{2,1,0:T(8,128)}, f32[18432,256]{1,0:T(8,128)}, f32[256,512]{1,0:T(8,128)}, f32[8,512]{1,0:T(8,128)}, f32[512,256]{...) custom-call(bf16[4,36,96,256]{3,2,1,0:T(8,128)(2,1)} %get-tuple-elem, ...), custom_call_target="tpu_custom_call" | custom-call | flops 31406948352 | bytes 113246208 | tf_op jit(solution)/shard_map/spectral_back_point_back/pallas_call | solution.py:1328
  641.2 145.3 %spectral_end.1 = (bf16[2,18432,256]{2,1,0:T(8,128)(2,1)}, f32[464,256]{1,0:T(8,128)}, f32[16,256]{1,0:T(8,128)}, bf16[18432,256]{1,0:T(8,128)(2,1)}) custom-call(bf16[4,36,96,256]{3,2,1,0:T(8,128)(2,1)} %get-tuple-element.99.refs_0_, bf16[4,672,256]{2,1,0:T(8,128)(2,1)} %get-tuple-element.100.refs_1_, ...), custom_call_target="tpu_custom_call", output_to_operand_aliasing={{0}: (28, {})} | custom-call | flops 3623878656 | bytes 84934656 | tf_op jit(solution)/shard_map/spectral_end/pallas_call | solution.py:1511
  786.5 21.4 %place.1 = (f32[1,2,18432,256]{3,2,1,0:T(8,128)}, f32[1,2,64]{2,1,0:T(2,128)}, f32[1,2,64]{2,1,0:T(2,128)}, f32[1,2,64,192]{3,2,1,0:T(8,128)}, f32[1,64,512]{2,1...) custom-call(s32[2]{0:T(128)} %pad_add_fusion.where, ...), custom_call_target="tpu_custom_call" | custom-call | tf_op jit(solution)/shard_map/place/pallas_call | solution.py:1626
  (3 shorter events, 0.0 us)
